TPU v7x, 32 devices: a whole 2x2x4 slice. The times are simulated.
32 devices in a mesh: groups: 2 (over y), expert: 4 (over z), dp: 2 (over x), mp: 2 (over core).
Axes of the slice: x: 2, y: 2, z: 4, core: 2. Of those that a mesh axis runs over, the one named last changes fastest.
Arguments:
- latent: float32 [512, 2048], P(('groups', 'expert', 'dp', 'mp')), parts along dimension 0, may hold values from -6 to 6
- time_embedding: float32 [2048], replicated, may hold values from -6 to 6
- norm_gain: float32 [2, 2048], replicated, may hold values from 0.1 to 1.9
- router: float32 [2, 2048, 16], replicated, may hold values from -0.03125 to 0.03125
- up_proj: bfloat16 [2, 16, 2048, 1408], P(None, 'expert', None, 'dp'), may hold values from -0.125 to 0.125
- down_proj: bfloat16 [2, 16, 1408, 2048], P(None, 'expert', 'dp'), may hold values from -0.15625 to 0.15625
- routes: int32 [2, 2, 512, 2], P(None, None, ('groups', 'expert', 'dp', 'mp')), parts along dimension 2, may hold values from 0 to 15, all different within a row; in each aligned block of 16 rows (0 to 15, 16 to 31, ..., all dimensions but the last counted through in order) at most 2 rows name the same one
Outputs:
- next_latent: float32 [512, 2048], P(('groups', 'expert', 'dp', 'mp')), parts along dimension 0
- mean_velocity: float32 [512, 2048], P(('groups', 'expert', 'dp', 'mp')), parts along dimension 0
There are 2 independent parts, one for each index of `groups`. A program takes and returns all parts, laid end to end along the dimension named above; an argument that names none is the same for every part. Nothing has to cross between parts.
Inputs may be any that keep to these rules, and one draw needn't show every extreme that they name: `routes`: in each evaluation and layer, the 16 tokens of one device (aligned blocks along the token dimension) name any one expert at most 2 times, a bound that some block reaches by one device's tokens; a token's two experts differ.
All inputs are finite; a program needn't handle non-finite values.
Results may differ from a plain program's by a relative error of at most 0.0055.
Values may be sent and summed in bfloat16 or wider, within the bound.
A program may use at most 128 MiB of HBM per device.

v0:
```python
import jax
import jax.numpy as jnp
from jax import lax
from jax.sharding import PartitionSpec as P

CAP = 2


epsilon = 1e-06
start_time = 1.0
step_size = -0.5


def local_block(state, gain, router_layer, up_layer, down_layer, chosen):
    tok_count = state.shape[0]
    model_width = state.shape[1]
    top_count = chosen.shape[1]
    experts = router_layer.shape[1]
    local_experts = up_layer.shape[0]
    inverse = lax.rsqrt(jnp.mean(state * state, axis=1, keepdims=True) + epsilon)
    scaled = state * inverse * gain[None, :]
    normed = scaled.astype(jnp.bfloat16)
    logits = jnp.dot(scaled, router_layer, precision=lax.Precision.HIGHEST)
    picked = jnp.take_along_axis(logits, chosen, axis=1)
    leading = jax.nn.sigmoid(picked[:, 0] - picked[:, 1])
    weights = jnp.stack([leading, 1.0 - leading], axis=1)
    flat_choice = chosen.reshape(-1)
    onehot = (flat_choice[:, None] == jnp.arange(experts, dtype=jnp.int32)[None, :]).astype(
        jnp.int32
    )
    before = jnp.cumsum(onehot, axis=0) - onehot
    position = jnp.sum(before * onehot, axis=1)
    slot_id = flat_choice * CAP + position
    targets = slot_id.reshape(tok_count, top_count)
    select = jnp.any(
        jnp.arange(experts * CAP, dtype=jnp.int32)[:, None, None] == targets[None, :, :], axis=2
    ).astype(jnp.bfloat16)
    buffer = (
        jnp.dot(select, normed, preferred_element_type=jnp.float32)
        .astype(jnp.bfloat16)
        .reshape(experts, CAP, model_width)
    )
    landed = lax.all_to_all(buffer, "expert", split_axis=0, concat_axis=0, tiled=True)
    arrived = lax.all_gather(landed[None], "dp", axis=0, tiled=True)
    group_count = arrived.shape[0]
    source_count = arrived.shape[1] // local_experts
    grouped = (
        arrived.reshape(group_count, source_count, local_experts, CAP, model_width)
        .transpose(2, 0, 1, 3, 4)
        .reshape(local_experts, group_count * source_count * CAP, model_width)
    )
    hidden = jax.nn.gelu(
        jnp.einsum("erd,edf->erf", grouped, up_layer, preferred_element_type=jnp.float32),
        approximate=True,
    ).astype(jnp.bfloat16)
    partial_value = jnp.einsum(
        "erf,efd->erd", hidden, down_layer, preferred_element_type=jnp.float32
    ).astype(jnp.bfloat16)
    partial_value = (
        partial_value.reshape(local_experts, group_count, source_count, CAP, model_width)
        .transpose(1, 2, 0, 3, 4)
        .reshape(group_count, source_count * local_experts, CAP, model_width)
    )
    owned = lax.all_to_all(partial_value, "dp", split_axis=0, concat_axis=0, tiled=True)
    summed = jnp.sum(owned.astype(jnp.float32), axis=0).astype(jnp.bfloat16)
    returned = lax.all_to_all(summed, "expert", split_axis=0, concat_axis=0, tiled=True)
    gathered = returned.reshape(experts * CAP, model_width)[slot_id].reshape(
        tok_count, top_count, model_width
    )
    return state + jnp.sum(weights[:, :, None] * gathered.astype(jnp.float32), axis=1)


def velocity(
    latent_now, time_now, section_routes, time_embedding, norm_gain, router, up_proj, down_proj
):
    state = latent_now + time_now * time_embedding[None, :]
    for layer_index in range(norm_gain.shape[0]):
        state = local_block(
            state,
            norm_gain[layer_index],
            router[layer_index],
            up_proj[layer_index],
            down_proj[layer_index],
            section_routes[layer_index],
        )
    return state - latent_now


def per_device(latent, time_embedding, norm_gain, router, up_proj, down_proj, routes):
    first = velocity(
        latent, start_time, routes[0], time_embedding, norm_gain, router, up_proj, down_proj
    )
    moved = latent + step_size * first
    second = velocity(
        moved,
        start_time + step_size,
        routes[1],
        time_embedding,
        norm_gain,
        router,
        up_proj,
        down_proj,
    )
    mean_velocity = 0.5 * (first + second)
    return (latent + step_size * mean_velocity, mean_velocity)


def solution(mesh):
    placed = (
        P(("groups", "expert", "dp", "mp"), None),
        P(),
        P(),
        P(),
        P(None, "expert", None, "dp"),
        P(None, "expert", "dp", None),
        P(None, None, ("groups", "expert", "dp", "mp"), None),
    )
    return jax.shard_map(
        per_device,
        mesh=mesh,
        in_specs=placed,
        out_specs=(
            P(("groups", "expert", "dp", "mp"), None),
            P(("groups", "expert", "dp", "mp"), None),
        ),
        check_vma=False,
    )
```

profile of v0, /device:TPU:0, one launch (start us, length us, event | category | flops | bytes accessed | tf_op | source)
XLA Modules:
  0.0 211.1 jit_solution(11158140217822368386)
XLA Ops:
  0.7 0.8 broadcast_multiply_fusion.2
  4.1 0.8 fusion.141
  5.0 1.0 multiply_reduce_fusion.7
  6.0 0.7 fusion.132
  6.8 1.1 convolution_convert_fusion.3
  8.0 0.8 reshape.307
  8.7 6.3 %all-to-all-start = ((bf16[16,2,2048]{2,1,0:T(2,128)(2,1)}), bf16[16,2,2048]{2,1,0:T(2,128)(2,1)S(1)}, u32[]{:S(2)}, u32[]{:S(2)}) async-start(bf16[16,2,2048]{2,1,0:T(2,128)(2,1)} %reshape.307), calls=%async_computation | async-start | bytes 262144 | tf_op jit(solution)/shard_map/all_to_all | solution.py:43
  15.1 0.7 bitcast_or_fusion
  16.0 1.3 fusion.90
  17.5 0.7 gather_fusion.4
  18.4 0.7 and_select_fusion.3
  19.7 1.4 all-to-all-done
  21.1 5.6 %all-gather = bf16[32,2,2048]{2,1,0:T(2,128)(2,1)S(1)} all-gather(bf16[16,2,2048]{2,1,0:T(2,128)(2,1)S(1)} %all-to-all-done), channel_id=2, replica_groups=mesh['groups'=2,'expert'=4,'dp'=2,'mp'=2] {'dp'}, dimensions={0}, use_global_device_ids=true | all-gather | bytes 393216 | tf_op jit(solution)/shard_map/all_gather | solution.py:44
  27.1 6.0 %fusion.45 = bf16[4,16,704]{2,1,0:T(8,128)(2,1)S(1)} fusion(bf16[4,16,2048]{2,1,0:T(8,128)(2,1)S(1)} %reshape.309, bf16[2,4,2048,704]{2,3,1,0:T(8,128)(2,1)} %param.13), kind=kOutput, calls=%fused_computation.59 | convolution fusion | flops 184954880 | bytes 11886592 | tf_op jit(solution)/shard_map/erd,edf->erf/dot_general | solution.py:53
  33.1 5.9 %fusion.24 = bf16[4,16,2048]{2,1,0:T(8,128)(2,1)S(1)} fusion(bf16[4,16,704]{2,1,0:T(8,128)(2,1)S(1)} %fusion.45, bf16[2,4,704,2048]{3,2,1,0:T(8,128)(2,1)} %param.14), kind=kOutput, calls=%fused_computation.32 | convolution fusion | flops 184680448 | bytes 11886592 | tf_op jit(solution)/shard_map/erf,efd->erd/dot_general | solution.py:56
  39.2 0.9 copy.119
  40.1 3.4 %all-to-all-start.1 = ((bf16[2,16,2,2048]{3,2,1,0:T(2,128)(2,1)}), bf16[2,16,2,2048]{3,2,1,0:T(2,128)(2,1)S(1)}, u32[]{:S(2)}, u32[]{:S(2)}) async-start(bf16[2,16,2,2048]{3,2,1,0:T(2,128)(2,1)} %bitcast.9), calls=%async_computation.1 | async-start | bytes 524288 | tf_op jit(solution)/shard_map/all_to_all | solution.py:64
  44.3 4.4 %all-to-all-done.1 = bf16[2,16,2,2048]{3,2,1,0:T(2,128)(2,1)S(1)} async-done(((bf16[2,16,2,2048]{3,2,1,0:T(2,128)(2,1)}), bf16[2,16,2,2048]{3,2,1,0:T(2,128)(2,1)S(1)}, u32[]{:S(2)}, u32[]{:S(2)}) %all-to-all-start.1) | async-done | bytes 262176 | tf_op jit(solution)/shard_map/all_to_all | solution.py:64
  48.7 1.2 reduce_sum.175
  49.9 3.7 %all-to-all-start.2 = ((bf16[16,2,2048]{2,1,0:T(2,128)(2,1)}), bf16[16,2,2048]{2,1,0:T(2,128)(2,1)S(1)}, u32[]{:S(2)}, u32[]{:S(2)}) async-start(bf16[16,2,2048]{2,1,0:T(2,128)(2,1)} %reduce_sum.175), calls=%async_computation.2 | async-start | bytes 262144 | tf_op jit(solution)/shard_map/all_to_all | solution.py:66
  53.6 5.9 %all-to-all-done.2 = bf16[16,2,2048]{2,1,0:T(2,128)(2,1)S(1)} async-done(((bf16[16,2,2048]{2,1,0:T(2,128)(2,1)}), bf16[16,2,2048]{2,1,0:T(2,128)(2,1)S(1)}, u32[]{:S(2)}, u32[]{:S(2)}) %all-to-all-start.2) | async-done | bytes 131104 | tf_op jit(solution)/shard_map/all_to_all | solution.py:66
  59.6 0.7 gather_fusion
  61.2 0.8 reshape.313
  62.0 3.3 %all-to-all-start.3 = ((bf16[16,2,2048]{2,1,0:T(2,128)(2,1)}), bf16[16,2,2048]{2,1,0:T(2,128)(2,1)S(1)}, u32[]{:S(2)}, u32[]{:S(2)}) async-start(bf16[16,2,2048]{2,1,0:T(2,128)(2,1)} %reshape.313), calls=%async_computation.3 | async-start | bytes 262144 | tf_op jit(solution)/shard_map/all_to_all | solution.py:43
  65.6 0.8 gather_fusion.5
  66.6 4.6 %all-to-all-done.3 = bf16[16,2,2048]{2,1,0:T(2,128)(2,1)S(1)} async-done(((bf16[16,2,2048]{2,1,0:T(2,128)(2,1)}), bf16[16,2,2048]{2,1,0:T(2,128)(2,1)S(1)}, u32[]{:S(2)}, u32[]{:S(2)}) %all-to-all-start.3) | async-done | bytes 131104 | tf_op jit(solution)/shard_map/all_to_all | solution.py:43
  71.2 5.6 %all-gather.1 = bf16[32,2,2048]{2,1,0:T(2,128)(2,1)S(1)} all-gather(bf16[16,2,2048]{2,1,0:T(2,128)(2,1)S(1)} %all-to-all-done.3), channel_id=3, replica_groups=mesh['groups'=2,'expert'=4,'dp'=2,'mp'=2] {'dp'}, dimensions={0}, use_global_device_ids=true | all-gather | bytes 393216 | tf_op jit(solution)/shard_map/all_gather | solution.py:44
  77.1 6.0 %fusion.57 = bf16[4,16,704]{2,1,0:T(8,128)(2,1)S(1)} fusion(bf16[4,16,2048]{2,1,0:T(8,128)(2,1)S(1)} %reshape.315, bf16[2,4,2048,704]{2,3,1,0:T(8,128)(2,1)} %param.13), kind=kOutput, calls=%fused_computation.67 | convolution fusion | flops 184954880 | bytes 11886592 | tf_op jit(solution)/shard_map/erd,edf->erf/dot_general | solution.py:53
  83.2 5.9 %fusion.30 = bf16[4,16,2048]{2,1,0:T(8,128)(2,1)S(1)} fusion(bf16[4,16,704]{2,1,0:T(8,128)(2,1)S(1)} %fusion.57, bf16[2,4,704,2048]{3,2,1,0:T(8,128)(2,1)} %param.14), kind=kOutput, calls=%fused_computation.34 | convolution fusion | flops 184680448 | bytes 11886592 | tf_op jit(solution)/shard_map/erf,efd->erd/dot_general | solution.py:56
  89.3 0.9 copy.127
  90.1 3.4 %all-to-all-start.4 = ((bf16[2,16,2,2048]{3,2,1,0:T(2,128)(2,1)}), bf16[2,16,2,2048]{3,2,1,0:T(2,128)(2,1)S(1)}, u32[]{:S(2)}, u32[]{:S(2)}) async-start(bf16[2,16,2,2048]{3,2,1,0:T(2,128)(2,1)} %bitcast.21), calls=%async_computation.4 | async-start | bytes 524288 | tf_op jit(solution)/shard_map/all_to_all | solution.py:64
  93.6 5.1 %all-to-all-done.4 = bf16[2,16,2,2048]{3,2,1,0:T(2,128)(2,1)S(1)} async-done(((bf16[2,16,2,2048]{3,2,1,0:T(2,128)(2,1)}), bf16[2,16,2,2048]{3,2,1,0:T(2,128)(2,1)S(1)}, u32[]{:S(2)}, u32[]{:S(2)}) %all-to-all-start.4) | async-done | bytes 262176 | tf_op jit(solution)/shard_map/all_to_all | solution.py:64
  98.8 1.2 reduce_sum.181
  99.9 3.5 %all-to-all-start.5 = ((bf16[16,2,2048]{2,1,0:T(2,128)(2,1)}), bf16[16,2,2048]{2,1,0:T(2,128)(2,1)S(1)}, u32[]{:S(2)}, u32[]{:S(2)}) async-start(bf16[16,2,2048]{2,1,0:T(2,128)(2,1)} %reduce_sum.181), calls=%async_computation.5 | async-start | bytes 262144 | tf_op jit(solution)/shard_map/all_to_all | solution.py:66
  103.6 5.6 %all-to-all-done.5 = bf16[16,2,2048]{2,1,0:T(2,128)(2,1)S(1)} async-done(((bf16[16,2,2048]{2,1,0:T(2,128)(2,1)}), bf16[16,2,2048]{2,1,0:T(2,128)(2,1)S(1)}, u32[]{:S(2)}, u32[]{:S(2)}) %all-to-all-start.5) | async-done | bytes 131104 | tf_op jit(solution)/shard_map/all_to_all | solution.py:66
  109.2 0.7 gather_fusion.1
  110.9 0.8 reshape.319
  111.6 3.3 %all-to-all-start.6 = ((bf16[16,2,2048]{2,1,0:T(2,128)(2,1)}), bf16[16,2,2048]{2,1,0:T(2,128)(2,1)S(1)}, u32[]{:S(2)}, u32[]{:S(2)}) async-start(bf16[16,2,2048]{2,1,0:T(2,128)(2,1)} %reshape.319), calls=%async_computation.6 | async-start | bytes 262144 | tf_op jit(solution)/shard_map/all_to_all | solution.py:43
  115.3 0.8 gather_fusion.6
  116.2 4.6 %all-to-all-done.6 = bf16[16,2,2048]{2,1,0:T(2,128)(2,1)S(1)} async-done(((bf16[16,2,2048]{2,1,0:T(2,128)(2,1)}), bf16[16,2,2048]{2,1,0:T(2,128)(2,1)S(1)}, u32[]{:S(2)}, u32[]{:S(2)}) %all-to-all-start.6) | async-done | bytes 131104 | tf_op jit(solution)/shard_map/all_to_all | solution.py:43
  120.8 5.6 %all-gather.2 = bf16[32,2,2048]{2,1,0:T(2,128)(2,1)S(1)} all-gather(bf16[16,2,2048]{2,1,0:T(2,128)(2,1)S(1)} %all-to-all-done.6), channel_id=4, replica_groups=mesh['groups'=2,'expert'=4,'dp'=2,'mp'=2] {'dp'}, dimensions={0}, use_global_device_ids=true | all-gather | bytes 393216 | tf_op jit(solution)/shard_map/all_gather | solution.py:44
  126.8 6.0 %fusion.69 = bf16[4,16,704]{2,1,0:T(8,128)(2,1)S(1)} fusion(bf16[4,16,2048]{2,1,0:T(8,128)(2,1)S(1)} %reshape.321, bf16[2,4,2048,704]{2,3,1,0:T(8,128)(2,1)} %param.13), kind=kOutput, calls=%fused_computation.75 | convolution fusion | flops 184954880 | bytes 11886592 | tf_op jit(solution)/shard_map/erd,edf->erf/dot_general | solution.py:53
  132.8 5.9 %fusion.27 = bf16[4,16,2048]{2,1,0:T(8,128)(2,1)S(1)} fusion(bf16[4,16,704]{2,1,0:T(8,128)(2,1)S(1)} %fusion.69, bf16[2,4,704,2048]{3,2,1,0:T(8,128)(2,1)} %param.14), kind=kOutput, calls=%fused_computation.33 | convolution fusion | flops 184680448 | bytes 11886592 | tf_op jit(solution)/shard_map/erf,efd->erd/dot_general | solution.py:56
  138.9 0.9 copy.135
  139.8 3.4 %all-to-all-start.7 = ((bf16[2,16,2,2048]{3,2,1,0:T(2,128)(2,1)}), bf16[2,16,2,2048]{3,2,1,0:T(2,128)(2,1)S(1)}, u32[]{:S(2)}, u32[]{:S(2)}) async-start(bf16[2,16,2,2048]{3,2,1,0:T(2,128)(2,1)} %bitcast.29), calls=%async_computation.7 | async-start | bytes 524288 | tf_op jit(solution)/shard_map/all_to_all | solution.py:64
  143.3 5.1 %all-to-all-done.7 = bf16[2,16,2,2048]{3,2,1,0:T(2,128)(2,1)S(1)} async-done(((bf16[2,16,2,2048]{3,2,1,0:T(2,128)(2,1)}), bf16[2,16,2,2048]{3,2,1,0:T(2,128)(2,1)S(1)}, u32[]{:S(2)}, u32[]{:S(2)}) %all-to-all-start.7) | async-done | bytes 262176 | tf_op jit(solution)/shard_map/all_to_all | solution.py:64
  148.4 1.2 reduce_sum.187
  149.6 3.3 %all-to-all-start.8 = ((bf16[16,2,2048]{2,1,0:T(2,128)(2,1)}), bf16[16,2,2048]{2,1,0:T(2,128)(2,1)S(1)}, u32[]{:S(2)}, u32[]{:S(2)}) async-start(bf16[16,2,2048]{2,1,0:T(2,128)(2,1)} %reduce_sum.187), calls=%async_computation.8 | async-start | bytes 262144 | tf_op jit(solution)/shard_map/all_to_all | solution.py:66
  153.0 5.8 %all-to-all-done.8 = bf16[16,2,2048]{2,1,0:T(2,128)(2,1)S(1)} async-done(((bf16[16,2,2048]{2,1,0:T(2,128)(2,1)}), bf16[16,2,2048]{2,1,0:T(2,128)(2,1)S(1)}, u32[]{:S(2)}, u32[]{:S(2)}) %all-to-all-start.8) | async-done | bytes 131104 | tf_op jit(solution)/shard_map/all_to_all | solution.py:66
  160.5 0.8 reshape.325
  161.2 3.3 %all-to-all-start.9 = ((bf16[16,2,2048]{2,1,0:T(2,128)(2,1)}), bf16[16,2,2048]{2,1,0:T(2,128)(2,1)S(1)}, u32[]{:S(2)}, u32[]{:S(2)}) async-start(bf16[16,2,2048]{2,1,0:T(2,128)(2,1)} %reshape.325), calls=%async_computation.9 | async-start | bytes 262144 | tf_op jit(solution)/shard_map/all_to_all | solution.py:43
  164.9 0.8 gather_fusion.7
  165.8 4.6 %all-to-all-done.9 = bf16[16,2,2048]{2,1,0:T(2,128)(2,1)S(1)} async-done(((bf16[16,2,2048]{2,1,0:T(2,128)(2,1)}), bf16[16,2,2048]{2,1,0:T(2,128)(2,1)S(1)}, u32[]{:S(2)}, u32[]{:S(2)}) %all-to-all-start.9) | async-done | bytes 131104 | tf_op jit(solution)/shard_map/all_to_all | solution.py:43
  170.5 5.6 %all-gather.3 = bf16[32,2,2048]{2,1,0:T(2,128)(2,1)S(1)} all-gather(bf16[16,2,2048]{2,1,0:T(2,128)(2,1)S(1)} %all-to-all-done.9), channel_id=5, replica_groups=mesh['groups'=2,'expert'=4,'dp'=2,'mp'=2] {'dp'}, dimensions={0}, use_global_device_ids=true | all-gather | bytes 393216 | tf_op jit(solution)/shard_map/all_gather | solution.py:44
  176.4 6.0 %fusion.81 = bf16[4,16,704]{2,1,0:T(8,128)(2,1)S(1)} fusion(bf16[4,16,2048]{2,1,0:T(8,128)(2,1)S(1)} %reshape.327, bf16[2,4,2048,704]{2,3,1,0:T(8,128)(2,1)} %param.13), kind=kOutput, calls=%fused_computation.83 | convolution fusion | flops 184954880 | bytes 11886592 | tf_op jit(solution)/shard_map/erd,edf->erf/dot_general | solution.py:53
  182.4 5.9 %fusion.33 = bf16[4,16,2048]{2,1,0:T(8,128)(2,1)S(1)} fusion(bf16[4,16,704]{2,1,0:T(8,128)(2,1)S(1)} %fusion.81, bf16[2,4,704,2048]{3,2,1,0:T(8,128)(2,1)} %param.14), kind=kOutput, calls=%fused_computation.35 | convolution fusion | flops 184680448 | bytes 11886592 | tf_op jit(solution)/shard_map/erf,efd->erd/dot_general | solution.py:56
  188.5 0.9 copy.143
  189.4 3.4 %all-to-all-start.10 = ((bf16[2,16,2,2048]{3,2,1,0:T(2,128)(2,1)}), bf16[2,16,2,2048]{3,2,1,0:T(2,128)(2,1)S(1)}, u32[]{:S(2)}, u32[]{:S(2)}) async-start(bf16[2,16,2,2048]{3,2,1,0:T(2,128)(2,1)} %bitcast.37), calls=%async_computation.10 | async-start | bytes 524288 | tf_op jit(solution)/shard_map/all_to_all | solution.py:64
  192.9 5.1 %all-to-all-done.10 = bf16[2,16,2,2048]{3,2,1,0:T(2,128)(2,1)S(1)} async-done(((bf16[2,16,2,2048]{3,2,1,0:T(2,128)(2,1)}), bf16[2,16,2,2048]{3,2,1,0:T(2,128)(2,1)S(1)}, u32[]{:S(2)}, u32[]{:S(2)}) %all-to-all-start.10) | async-done | bytes 262176 | tf_op jit(solution)/shard_map/all_to_all | solution.py:64
  198.0 1.2 reduce_sum.193
  199.2 3.3 %all-to-all-start.11 = ((bf16[16,2,2048]{2,1,0:T(2,128)(2,1)}), bf16[16,2,2048]{2,1,0:T(2,128)(2,1)S(1)}, u32[]{:S(2)}, u32[]{:S(2)}) async-start(bf16[16,2,2048]{2,1,0:T(2,128)(2,1)} %reduce_sum.193), calls=%async_computation.11 | async-start | bytes 262144 | tf_op jit(solution)/shard_map/all_to_all | solution.py:66
  202.6 5.8 %all-to-all-done.11 = bf16[16,2,2048]{2,1,0:T(2,128)(2,1)S(1)} async-done(((bf16[16,2,2048]{2,1,0:T(2,128)(2,1)}), bf16[16,2,2048]{2,1,0:T(2,128)(2,1)S(1)}, u32[]{:S(2)}, u32[]{:S(2)}) %all-to-all-start.11) | async-done | bytes 131104 | tf_op jit(solution)/shard_map/all_to_all | solution.py:66
  209.7 0.7 broadcast_multiply_fusion
  210.4 0.7 multiply_add_fusion
  (125 shorter events, 13.2 us)
Async XLA Ops:
  0.6 53.0 %copy-start.2 = (f32[2048]{0:T(1024)S(1)}, f32[2048]{0:T(1024)}, u32[]{:S(2)}) copy-start(f32[2048]{0:T(1024)} %param.10) | copy-start | bytes 24580
  0.6 60.2 %copy-start = (f32[16,2048]{1,0:T(8,128)S(1)}, f32[16,2048]{1,0:T(8,128)}, u32[]{:S(2)}) copy-start(f32[16,2048]{1,0:T(8,128)} %param.9) | copy-start | bytes 393220
  0.7 64.7 %copy-start.1 = (f32[2,2048,16]{1,2,0:T(8,128)S(1)}, f32[2,2048,16]{1,2,0:T(8,128)}, u32[]{:S(2)}) copy-start(f32[2,2048,16]{1,2,0:T(8,128)} %param.12) | copy-start | bytes 786436
  8.7 12.4 %all-to-all-start = ((bf16[16,2,2048]{2,1,0:T(2,128)(2,1)}), bf16[16,2,2048]{2,1,0:T(2,128)(2,1)S(1)}, u32[]{:S(2)}, u32[]{:S(2)}) async-start(bf16[16,2,2048]{2,1,0:T(2,128)(2,1)} %reshape.307), calls=%async_computation | async-start | bytes 262144 | tf_op jit(solution)/shard_map/all_to_all | solution.py:43
  39.0 54.6 %copy-start.3 = (s32[2,2,16,2]{2,3,1,0:T(2,128)S(1)}, s32[2,2,16,2]{2,3,1,0:T(2,128)}, u32[]{:S(2)}) copy-start(s32[2,2,16,2]{2,3,1,0:T(2,128)} %param.15) | copy-start | bytes 1540
  40.1 8.6 %all-to-all-start.1 = ((bf16[2,16,2,2048]{3,2,1,0:T(2,128)(2,1)}), bf16[2,16,2,2048]{3,2,1,0:T(2,128)(2,1)S(1)}, u32[]{:S(2)}, u32[]{:S(2)}) async-start(bf16[2,16,2,2048]{3,2,1,0:T(2,128)(2,1)} %bitcast.9), calls=%async_computation.1 | async-start | bytes 524288 | tf_op jit(solution)/shard_map/all_to_all | solution.py:64
  49.9 9.6 %all-to-all-start.2 = ((bf16[16,2,2048]{2,1,0:T(2,128)(2,1)}), bf16[16,2,2048]{2,1,0:T(2,128)(2,1)S(1)}, u32[]{:S(2)}, u32[]{:S(2)}) async-start(bf16[16,2,2048]{2,1,0:T(2,128)(2,1)} %reduce_sum.175), calls=%async_computation.2 | async-start | bytes 262144 | tf_op jit(solution)/shard_map/all_to_all | solution.py:66
  62.0 9.2 %all-to-all-start.3 = ((bf16[16,2,2048]{2,1,0:T(2,128)(2,1)}), bf16[16,2,2048]{2,1,0:T(2,128)(2,1)S(1)}, u32[]{:S(2)}, u32[]{:S(2)}) async-start(bf16[16,2,2048]{2,1,0:T(2,128)(2,1)} %reshape.313), calls=%async_computation.3 | async-start | bytes 262144 | tf_op jit(solution)/shard_map/all_to_all | solution.py:43
  90.1 8.6 %all-to-all-start.4 = ((bf16[2,16,2,2048]{3,2,1,0:T(2,128)(2,1)}), bf16[2,16,2,2048]{3,2,1,0:T(2,128)(2,1)S(1)}, u32[]{:S(2)}, u32[]{:S(2)}) async-start(bf16[2,16,2,2048]{3,2,1,0:T(2,128)(2,1)} %bitcast.21), calls=%async_computation.4 | async-start | bytes 524288 | tf_op jit(solution)/shard_map/all_to_all | solution.py:64
  99.9 9.2 %all-to-all-start.5 = ((bf16[16,2,2048]{2,1,0:T(2,128)(2,1)}), bf16[16,2,2048]{2,1,0:T(2,128)(2,1)S(1)}, u32[]{:S(2)}, u32[]{:S(2)}) async-start(bf16[16,2,2048]{2,1,0:T(2,128)(2,1)} %reduce_sum.181), calls=%async_computation.5 | async-start | bytes 262144 | tf_op jit(solution)/shard_map/all_to_all | solution.py:66
  111.6 9.2 %all-to-all-start.6 = ((bf16[16,2,2048]{2,1,0:T(2,128)(2,1)}), bf16[16,2,2048]{2,1,0:T(2,128)(2,1)S(1)}, u32[]{:S(2)}, u32[]{:S(2)}) async-start(bf16[16,2,2048]{2,1,0:T(2,128)(2,1)} %reshape.319), calls=%async_computation.6 | async-start | bytes 262144 | tf_op jit(solution)/shard_map/all_to_all | solution.py:43
  139.8 8.6 %all-to-all-start.7 = ((bf16[2,16,2,2048]{3,2,1,0:T(2,128)(2,1)}), bf16[2,16,2,2048]{3,2,1,0:T(2,128)(2,1)S(1)}, u32[]{:S(2)}, u32[]{:S(2)}) async-start(bf16[2,16,2,2048]{3,2,1,0:T(2,128)(2,1)} %bitcast.29), calls=%async_computation.7 | async-start | bytes 524288 | tf_op jit(solution)/shard_map/all_to_all | solution.py:64
  149.6 9.2 %all-to-all-start.8 = ((bf16[16,2,2048]{2,1,0:T(2,128)(2,1)}), bf16[16,2,2048]{2,1,0:T(2,128)(2,1)S(1)}, u32[]{:S(2)}, u32[]{:S(2)}) async-start(bf16[16,2,2048]{2,1,0:T(2,128)(2,1)} %reduce_sum.187), calls=%async_computation.8 | async-start | bytes 262144 | tf_op jit(solution)/shard_map/all_to_all | solution.py:66
  161.2 9.2 %all-to-all-start.9 = ((bf16[16,2,2048]{2,1,0:T(2,128)(2,1)}), bf16[16,2,2048]{2,1,0:T(2,128)(2,1)S(1)}, u32[]{:S(2)}, u32[]{:S(2)}) async-start(bf16[16,2,2048]{2,1,0:T(2,128)(2,1)} %reshape.325), calls=%async_computation.9 | async-start | bytes 262144 | tf_op jit(solution)/shard_map/all_to_all | solution.py:43
  189.4 8.6 %all-to-all-start.10 = ((bf16[2,16,2,2048]{3,2,1,0:T(2,128)(2,1)}), bf16[2,16,2,2048]{3,2,1,0:T(2,128)(2,1)S(1)}, u32[]{:S(2)}, u32[]{:S(2)}) async-start(bf16[2,16,2,2048]{3,2,1,0:T(2,128)(2,1)} %bitcast.37), calls=%async_computation.10 | async-start | bytes 524288 | tf_op jit(solution)/shard_map/all_to_all | solution.py:64
  199.2 9.2 %all-to-all-start.11 = ((bf16[16,2,2048]{2,1,0:T(2,128)(2,1)}), bf16[16,2,2048]{2,1,0:T(2,128)(2,1)S(1)}, u32[]{:S(2)}, u32[]{:S(2)}) async-start(bf16[16,2,2048]{2,1,0:T(2,128)(2,1)} %reduce_sum.193), calls=%async_computation.11 | async-start | bytes 262144 | tf_op jit(solution)/shard_map/all_to_all | solution.py:66
where the time goes:
time: 213 us; the launch traced here: 211 us
  waiting for transfers between devices  58.3 us (27%)
  matrix products  51.7 us (24%)
  starting transfers between devices  43.9 us (21%)
  blocking collectives  22.5 us (11%)
  local copies, waits for them, and re-layouts  19.8 us (9%)
  other arithmetic  13.6 us (6%)
    dot_general x4, matrix products, local_block(): jnp.einsum('erd,edf->erf', grouped, up_layer, preferred_element_type=jnp....  24.1 us
    dot_general x4, matrix products, local_block(): jnp.einsum('erf,efd->erd', hidden, down_layer, preferred_element_type=jnp...  23.6 us
    all_to_all x4, waiting for transfers between devices, local_block(): lax.all_to_all(summed, 'expert', split_axis=0, concat_axis=0, tiled=True)  23.1 us
    all_gather x4, blocking collectives, local_block(): arrived = lax.all_gather(landed[None], 'dp', axis=0, tiled=True)  22.5 us
    all_to_all x4, waiting for transfers between devices, local_block(): lax.all_to_all(partial_value, 'dp', split_axis=0, concat_axis=0, tiled=True)  19.9 us
    all_to_all x4, starting transfers between devices, local_block(): lax.all_to_all(buffer, 'expert', split_axis=0, concat_axis=0, tiled=True)  16.3 us
    all_to_all x4, waiting for transfers between devices, local_block(): lax.all_to_all(buffer, 'expert', split_axis=0, concat_axis=0, tiled=True)  15.3 us
    all_to_all x4, starting transfers between devices, local_block(): lax.all_to_all(summed, 'expert', split_axis=0, concat_axis=0, tiled=True)  13.9 us
  transfers between devices with their start and end apart: 12, of which 12 were waited for; matrix products, arithmetic and copies ran while one was open for 4% of the time, Pallas kernels for 0%

commit v1 on v0

--- a/solution.py
+++ b/solution.py
@@ -1,6 +1,9 @@
+import functools
 import jax
 import jax.numpy as jnp
 from jax import lax
+from jax.experimental import pallas as pl
+from jax.experimental.pallas import tpu as pltpu
 from jax.sharding import PartitionSpec as P
 
 CAP = 2
@@ -86,7 +89,7 @@
     return state - latent_now
 
 
-def per_device(latent, time_embedding, norm_gain, router, up_proj, down_proj, routes):
+def per_device_general(latent, time_embedding, norm_gain, router, up_proj, down_proj, routes):
     first = velocity(
         latent, start_time, routes[0], time_embedding, norm_gain, router, up_proj, down_proj
     )
@@ -105,6 +108,353 @@
     return (latent + step_size * mean_velocity, mean_velocity)
 
 
+PACK = 16
+BLOCKS = PACK // CAP
+MESH = pl.DeviceIdType.MESH
+
+
+def kernel(
+    sizes,
+    latent_ref, te_ref, gain_ref, router_hbm, up_hbm, down_hbm, routes_ref,
+    out_ref,
+    up_v, down_v, router_v, base, state, total,
+    take_first, take_second, spread, unpack, pack,
+    dsend, xbuf, ybuf, yrecv, zsend, rbuf,
+    w_sem, router_sem, d_send, d_recv, f_send, f_recv, y_send, y_recv, r_send, r_recv,
+):
+    nz, nc, layers, per_core, toks, width = sizes
+    cols = width // BLOCKS
+    srcs = 2 * nz * nc
+    half = nz * nc
+    z = lax.axis_index("expert")
+    x = lax.axis_index("dp")
+    c = lax.axis_index("mp")
+
+    def weight_copies(layer, j):
+        mine = c * per_core + j
+        return (
+            pltpu.make_async_copy(up_hbm.at[layer, mine], up_v.at[layer, j], w_sem.at[layer, j, 0]),
+            pltpu.make_async_copy(
+                down_hbm.at[layer, mine], down_v.at[layer, j], w_sem.at[layer, j, 1]
+            ),
+        )
+
+    router_copy = pltpu.make_async_copy(router_hbm, router_v, router_sem)
+    for layer in range(layers):
+        for j in range(per_core):
+            for copy in weight_copies(layer, j):
+                copy.start()
+        if layer == 0:
+            router_copy.start()
+
+    barrier = pltpu.get_barrier_semaphore()
+    others = [(dz, dc) for dz in range(nz) for dc in range(nc) if (dz, dc) != (0, 0)]
+    for dz, dc in others:
+        pl.semaphore_signal(
+            barrier, inc=1, device_id={"expert": lax.rem(z + dz, nz), "mp": lax.rem(c + dc, nc)},
+            device_id_type=MESH,
+        )
+    pl.semaphore_signal(barrier, inc=1, device_id={"dp": 1 - x}, device_id_type=MESH)
+
+    def places(rows, lanes, target):
+        lane = lax.broadcasted_iota(jnp.int32, (rows, lanes), 1)
+        return jnp.where(lane == target, 1.0, 0.0)
+
+    rows_in = srcs * PACK
+    per_block = srcs * CAP
+    i = lax.broadcasted_iota(jnp.int32, (rows_in, 1), 0)
+    unpack[...] = places(
+        rows_in, rows_in, (i % per_block) // CAP * PACK + i // per_block * CAP + i % CAP
+    ).astype(jnp.bfloat16)
+    back = half * PACK
+    i = lax.broadcasted_iota(jnp.int32, (back, 1), 0)
+    pack[...] = places(
+        back, back, (i % PACK) // CAP * (half * CAP) + i // PACK * CAP + i % CAP
+    ).astype(jnp.bfloat16)
+    experts = nz * nc * per_core
+
+    def route(p, carry):
+        chosen = routes_ref[p // layers, p % layers]
+        first, second = chosen[:, 0:1], chosen[:, 1:2]
+        lane = lax.broadcasted_iota(jnp.int32, (toks, 128), 1)
+        one = jnp.where(lane == first, 1.0, 0.0)
+        two = jnp.where(lane == second, 1.0, 0.0)
+        earlier = jnp.where(
+            lax.broadcasted_iota(jnp.int32, (toks, toks), 0)
+            > lax.broadcasted_iota(jnp.int32, (toks, toks), 1), 1.0, 0.0,
+        )
+        position = jnp.dot(
+            earlier.astype(jnp.bfloat16), (one + two).astype(jnp.bfloat16),
+            preferred_element_type=jnp.float32,
+        )
+        at_first = first * PACK + jnp.sum(position * one, axis=1, keepdims=True).astype(jnp.int32)
+        at_second = second * PACK + jnp.sum(position * two, axis=1, keepdims=True).astype(jnp.int32)
+        block = lax.broadcasted_iota(jnp.int32, (BLOCKS * toks, 1), 0) // toks * CAP
+        g0 = places(BLOCKS * toks, experts * PACK, jnp.concatenate([at_first] * BLOCKS, 0) + block)
+        g1 = places(BLOCKS * toks, experts * PACK, jnp.concatenate([at_second] * BLOCKS, 0) + block)
+        take_first[p] = g0.astype(jnp.bfloat16)
+        take_second[p] = g1.astype(jnp.bfloat16)
+        spread[p] = jnp.transpose(g0 + g1).astype(jnp.bfloat16)
+        return carry
+
+    lax.fori_loop(0, 2 * layers, route, 0)
+    base[...] = latent_ref[...]
+    pl.semaphore_wait(barrier, len(others) + 1)
+    router_copy.wait()
+
+    def dispatch_copy(j, dz, dc, src_z, src_c):
+        to_z, to_c = lax.rem(src_z + dz, nz), lax.rem(src_c + dc, nc)
+        expert = (to_z * nc + to_c) * per_core + j
+        return pltpu.make_async_remote_copy(
+            src_ref=dsend.at[pl.ds(pl.multiple_of(expert * PACK, PACK), PACK)],
+            dst_ref=xbuf.at[
+                j, pl.ds(pl.multiple_of(((x * nz + src_z) * nc + src_c) * PACK, PACK), PACK)
+            ],
+            send_sem=d_send.at[j, dz, dc],
+            recv_sem=d_recv.at[j, dz, dc],
+            device_id={"expert": to_z, "mp": to_c},
+            device_id_type=MESH,
+        )
+
+    def forward_copy(j, dz, side):
+        src_z = lax.rem(z + nz - dz, nz)
+        rows = pl.ds(pl.multiple_of((side * nz + src_z) * nc * PACK, nc * PACK), nc * PACK)
+        return pltpu.make_async_remote_copy(
+            src_ref=xbuf.at[j, rows],
+            dst_ref=xbuf.at[j, rows],
+            send_sem=f_send.at[j, dz],
+            recv_sem=f_recv.at[j, dz],
+            device_id={"dp": 1 - x},
+            device_id_type=MESH,
+        )
+
+    def result_copy(j):
+        return pltpu.make_async_remote_copy(
+            src_ref=ybuf.at[j, 1 - x],
+            dst_ref=yrecv.at[j],
+            send_sem=y_send.at[j],
+            recv_sem=y_recv.at[j],
+            device_id={"dp": 1 - x},
+            device_id_type=MESH,
+        )
+
+    def return_copy(j, dz, dc, src_z, src_c):
+        to_z, to_c = lax.rem(src_z + dz, nz), lax.rem(src_c + dc, nc)
+        expert = (src_z * nc + src_c) * per_core + j
+        return pltpu.make_async_remote_copy(
+            src_ref=zsend.at[j, pl.ds(pl.multiple_of((to_z * nc + to_c) * PACK, PACK), PACK)],
+            dst_ref=rbuf.at[pl.ds(pl.multiple_of(expert * PACK, PACK), PACK)],
+            send_sem=r_send.at[j, dz, dc],
+            recv_sem=r_recv.at[j, dz, dc],
+            device_id={"expert": to_z, "mp": to_c},
+            device_id_type=MESH,
+        )
+
+    def came_from(dz, dc):
+        return lax.rem(z + nz - dz, nz), lax.rem(c + nc - dc, nc)
+
+    def step(p, carry):
+        layer = lax.rem(p, layers)
+        evaluation = p // layers
+
+        @pl.when(layer == 0)
+        def _():
+            now = jnp.where(evaluation == 0, start_time, start_time + step_size)
+            state[...] = base[...] + now * te_ref[...]
+
+        old = state[...]
+        inverse = lax.rsqrt(jnp.mean(old * old, axis=1, keepdims=True) + epsilon)
+        scaled = old * inverse * gain_ref[pl.ds(layer, 1), :]
+        normed = scaled.astype(jnp.bfloat16)
+        stacked = jnp.concatenate(
+            [normed[:, b * cols:(b + 1) * cols] for b in range(BLOCKS)], axis=0
+        )
+        dsend[...] = jnp.dot(
+            spread[p], stacked, preferred_element_type=jnp.float32
+        ).astype(jnp.bfloat16)
+        for j in range(per_core):
+            for dz, dc in others:
+                dispatch_copy(j, dz, dc, z, c).start()
+        for j in range(per_core):
+            expert = (z * nc + c) * per_core + j
+            xbuf[j, pl.ds(pl.multiple_of(((x * nz + z) * nc + c) * PACK, PACK), PACK)] = dsend[
+                pl.ds(pl.multiple_of(expert * PACK, PACK), PACK)
+            ]
+
+        logits = jnp.dot(
+            scaled, router_v[layer], precision=lax.Precision.HIGHEST,
+            preferred_element_type=jnp.float32,
+        )
+        chosen = routes_ref[evaluation, layer]
+        lane = lax.broadcasted_iota(jnp.int32, logits.shape, 1)
+        of_first = jnp.sum(jnp.where(lane == chosen[:, 0:1], logits, 0.0), axis=1, keepdims=True)
+        of_second = jnp.sum(jnp.where(lane == chosen[:, 1:2], logits, 0.0), axis=1, keepdims=True)
+        mix0 = jax.nn.sigmoid(of_first - of_second)
+        mix1 = 1.0 - mix0
+
+        for j in range(per_core):
+            for dz in range(nz):
+                for dc in range(nc):
+                    if (dz, dc) != (0, 0):
+                        dispatch_copy(j, dz, dc, *came_from(dz, dc)).wait_recv()
+                forward_copy(j, dz, x).start()
+
+        for j in range(per_core):
+            for dz in range(nz):
+                forward_copy(j, dz, 1 - x).wait_recv()
+
+            @pl.when(evaluation == 0)
+            def _():
+                for copy in weight_copies(layer, j):
+                    copy.wait()
+
+            rows = jnp.dot(
+                unpack[...], xbuf[j], preferred_element_type=jnp.float32
+            ).astype(jnp.bfloat16)
+            acc = jnp.dot(
+                rows[:per_block], up_v[layer, j, :cols, :], preferred_element_type=jnp.float32
+            )
+            for b in range(1, BLOCKS):
+                acc += jnp.dot(
+                    rows[b * per_block:(b + 1) * per_block],
+                    up_v[layer, j, b * cols:(b + 1) * cols, :],
+                    preferred_element_type=jnp.float32,
+                )
+            hidden = jax.nn.gelu(acc, approximate=True).astype(jnp.bfloat16)
+            out = jnp.dot(
+                hidden, down_v[layer, j], preferred_element_type=jnp.float32
+            ).astype(jnp.bfloat16)
+            ybuf[j, 0] = out[:per_block // 2]
+            ybuf[j, 1] = out[per_block // 2:]
+            result_copy(j).start()
+
+        for j in range(per_core):
+            for dz in range(nz):
+                forward_copy(j, dz, x).wait_send()
+        for j in range(per_core):
+            result_copy(j).wait_recv()
+            summed = (
+                ybuf[j, x].astype(jnp.float32) + yrecv[j].astype(jnp.float32)
+            ).astype(jnp.bfloat16)
+            tall = jnp.concatenate(
+                [summed[:, b * cols:(b + 1) * cols] for b in range(BLOCKS)], axis=0
+            )
+            zsend[j] = jnp.dot(
+                pack[...], tall, preferred_element_type=jnp.float32
+            ).astype(jnp.bfloat16)
+            for dz, dc in others:
+                return_copy(j, dz, dc, z, c).start()
+            expert = (z * nc + c) * per_core + j
+            rbuf[pl.ds(pl.multiple_of(expert * PACK, PACK), PACK)] = zsend[
+                j, pl.ds(pl.multiple_of((z * nc + c) * PACK, PACK), PACK)
+            ]
+
+        for j in range(per_core):
+            result_copy(j).wait_send()
+            for dz, dc in others:
+                dispatch_copy(j, dz, dc, z, c).wait_send()
+        for j in range(per_core):
+            for dz, dc in others:
+                return_copy(j, dz, dc, *came_from(dz, dc)).wait_recv()
+        returned = rbuf[...]
+        g0 = jnp.dot(take_first[p], returned, preferred_element_type=jnp.float32)
+        g1 = jnp.dot(take_second[p], returned, preferred_element_type=jnp.float32)
+        for b in range(BLOCKS):
+            r = slice(b * toks, (b + 1) * toks)
+            w = slice(b * cols, (b + 1) * cols)
+            state[:, w] = old[:, w] + (mix0 * g0[r] + mix1 * g1[r])
+        for j in range(per_core):
+            for dz, dc in others:
+                return_copy(j, dz, dc, z, c).wait_send()
+
+        @pl.when(p == layers - 1)
+        def _():
+            first = state[...] - base[...]
+            total[...] = first
+            base[...] = base[...] + step_size * first
+
+        return carry
+
+    lax.fori_loop(0, 2 * layers, step, 0)
+    out_ref[...] = total[...] + (state[...] - base[...])
+
+
+def per_device(mesh_shape, latent, time_embedding, norm_gain, router, up_proj, down_proj, routes):
+    nz, nc = mesh_shape["expert"], mesh_shape["mp"]
+    layers, local_experts, width, hidden = up_proj.shape
+    experts = router.shape[2]
+    toks = latent.shape[0]
+    fits = (
+        mesh_shape["dp"] == 2
+        and local_experts % nc == 0
+        and local_experts * nz == experts
+        and local_experts // nc <= 2
+        and toks % 16 == 0
+        and width % (BLOCKS * 128) == 0
+        and hidden % 16 == 0
+        and (nz * nc * CAP) % 16 == 0
+        and routes.shape[0] == 2
+    )
+    if not fits:
+        return per_device_general(
+            latent, time_embedding, norm_gain, router, up_proj, down_proj, routes
+        )
+    per_core = local_experts // nc
+    cols = width // BLOCKS
+    srcs = 2 * nz * nc
+    half = nz * nc
+    bf16, f32 = jnp.bfloat16, jnp.float32
+    vmem = pl.BlockSpec(memory_space=pltpu.VMEM)
+    hbm = pl.BlockSpec(memory_space=pl.ANY)
+    dma = pltpu.SemaphoreType.DMA
+    flops = 2 * layers * per_core * srcs * CAP * width * hidden * 4
+    total = pl.pallas_call(
+        functools.partial(kernel, (nz, nc, layers, per_core, toks, width)),
+        out_shape=jax.ShapeDtypeStruct((toks, width), f32),
+        in_specs=[vmem, vmem, vmem, hbm, hbm, hbm, vmem],
+        out_specs=vmem,
+        scratch_shapes=[
+            pltpu.VMEM((layers, per_core, width, hidden), bf16),
+            pltpu.VMEM((layers, per_core, hidden, width), bf16),
+            pltpu.VMEM((layers, width, experts), f32),
+            pltpu.VMEM((toks, width), f32),
+            pltpu.VMEM((toks, width), f32),
+            pltpu.VMEM((toks, width), f32),
+            pltpu.VMEM((2 * layers, BLOCKS * toks, experts * PACK), bf16),
+            pltpu.VMEM((2 * layers, BLOCKS * toks, experts * PACK), bf16),
+            pltpu.VMEM((2 * layers, experts * PACK, BLOCKS * toks), bf16),
+            pltpu.VMEM((srcs * PACK, srcs * PACK), bf16),
+            pltpu.VMEM((half * PACK, half * PACK), bf16),
+            pltpu.VMEM((experts * PACK, cols), bf16),
+            pltpu.VMEM((per_core, srcs * PACK, cols), bf16),
+            pltpu.VMEM((per_core, 2, half * CAP, width), bf16),
+            pltpu.VMEM((per_core, half * CAP, width), bf16),
+            pltpu.VMEM((per_core, half * PACK, cols), bf16),
+            pltpu.VMEM((experts * PACK, cols), bf16),
+            dma((layers, per_core, 2)),
+            dma,
+            dma((per_core, nz, nc)),
+            dma((per_core, nz, nc)),
+            dma((per_core, nz)),
+            dma((per_core, nz)),
+            dma((per_core,)),
+            dma((per_core,)),
+            dma((per_core, nz, nc)),
+            dma((per_core, nz, nc)),
+        ],
+        compiler_params=pltpu.CompilerParams(
+            collective_id=0, has_side_effects=True, vmem_limit_bytes=56 * 1024 * 1024
+        ),
+        cost_estimate=pl.CostEstimate(
+            flops=flops,
+            bytes_accessed=layers * per_core * width * hidden * 4,
+            transcendentals=0,
+        ),
+    )(latent, time_embedding.reshape(1, width), norm_gain, router, up_proj, down_proj, routes)
+    mean_velocity = 0.5 * total
+    return (latent + step_size * mean_velocity, mean_velocity)
+
+
 def solution(mesh):
     placed = (
         P(("groups", "expert", "dp", "mp"), None),
@@ -116,7 +466,7 @@
         P(None, None, ("groups", "expert", "dp", "mp"), None),
     )
     return jax.shard_map(
-        per_device,
+        functools.partial(per_device, dict(mesh.shape)),
         mesh=mesh,
         in_specs=placed,
         out_specs=(

time: 213 us -> 122 us (0.57)
  Pallas kernels: 0 us -> 84 us
  waiting for transfers between devices: 58.3 us -> 0 us
  matrix products: 51.7 us -> 0 us
  starting transfers between devices: 43.9 us -> 0 us
  blocking collectives: 22.5 us -> 0 us
  local copies, waits for them, and re-layouts: 19.8 us -> 34.9 us
  other arithmetic: 13.6 us -> 1.62 us
    pallas_call x0 -> x1, Pallas kernels: none -> 84 us  [per_device(): pl.pallas_call(functools.partial(kernel, (nz, nc, layers, per_core, toks,...]
    all_to_all x12 -> x0, waiting for transfers between devices: 58.3 us -> none  [the longest x4 23.1 us: local_block(): lax.all_to_all(summed, 'expert', split_axis=0, concat_axis=0, tiled=True)]
    dot_general x16 -> x0, matrix products: 51.7 us -> none  [the longest x4 24.1 us: local_block(): jnp.einsum('erd,edf->erf', grouped, up_layer, preferred_element_type=jnp....]
    all_to_all x12 -> x0, starting transfers between devices: 43.9 us -> none  [the longest x4 16.3 us: local_block(): lax.all_to_all(buffer, 'expert', split_axis=0, concat_axis=0, tiled=True)]
    unnamed x8 -> x5, local copies, waits for them, and re-layouts: 0.02 us -> 34.9 us
    all_gather x4 -> x0, blocking collectives: 22.5 us -> none  [local_block(): arrived = lax.all_gather(landed[None], 'dp', axis=0, tiled=True)]
    reshape x24 -> x0, local copies, waits for them, and re-layouts: 8.75 us -> none  [the longest x8 4.33 us: local_block(): partial_value.reshape(local_experts, group_count, source_count, CAP, mode...]
    reduce_sum x16 -> x0, other arithmetic: 8.44 us -> none  [the longest x4 4.68 us: local_block(): summed = jnp.sum(owned.astype(jnp.float32), axis=0).astype(jnp.bfloat16)]
  transfers between devices with their start and end apart: 12 -> 0, of which waited for: 12 -> 0; matrix products, arithmetic and copies ran while one was open for 4% -> 0% of each run, Pallas kernels for 0% -> 0%
where the time goes in v1:
time: 122 us; the launch traced here: 121 us
  Pallas kernels  84 us (69%)
  local copies, waits for them, and re-layouts  34.9 us (29%)
  other arithmetic  1.62 us (1%)
    pallas_call x1, Pallas kernels, per_device(): pl.pallas_call(functools.partial(kernel, (nz, nc, layers, per_core, toks,...  84 us
    unnamed x5, local copies, waits for them, and re-layouts  34.9 us

profile of v1, /device:TPU:0, one launch (start us, length us, event | category | flops | bytes accessed | tf_op | source)
XLA Modules:
  0.0 121.1 jit_solution(14188815082078170274)
XLA Ops:
  0.6 1.4 %copy.11.routes_ref = s32[2,2,16,2]{3,2,1,0:T(8,128)} copy(s32[2,2,16,2]{2,3,1,0:T(2,128)} %param.13) | data formatting | bytes 1024 | tf_op args[6]
  2.0 2.9 %copy.9.router_hbm = f32[2,2048,16]{2,1,0:T(8,128)} copy(f32[2,2048,16]{1,2,0:T(8,128)} %param.10) | data formatting | bytes 524288 | tf_op args[3]
  5.0 30.5 %copy.10.up_hbm = bf16[2,4,2048,704]{3,2,1,0:T(8,128)(2,1)} copy(bf16[2,4,2048,704]{2,3,1,0:T(8,128)(2,1)} %param.11) | data formatting | bytes 46137344 | tf_op args[4]
  35.5 0.0 copy-start
  35.5 84.0 %shard_map.86 = f32[16,2048]{1,0:T(8,128)} custom-call(f32[16,2048]{1,0:T(8,128)} %latent_ref.1, f32[1,2048]{1,0:T(1,128)} %bitcast.1, f32[2,2048]{1,0:T(2,128)} %gain_ref.1, f32[2,2048,16]{2,1,0:T(8,128)} %copy.9.router_hbm, bf16[2,4,2048,704]{3,2,1,0:T(8,128)(2,1)} %copy.10.up_hbm, bf16[2,4,704,2048]{3,2,1,0:T(8,128)(2,1)} %down_hbm.1, ...), custom_call_target="tpu_custom_call" | custom-call | flops 1476395008 | bytes 23068672 | tf_op jit(solution)/shard_map/pallas_call | solution.py:411
  119.5 0.0 copy-done
  119.5 1.6 %broadcast_multiply_fusion = (f32[16,2048]{1,0:T(8,128)}, f32[16,2048]{1,0:T(8,128)}) fusion(f32[16,2048]{1,0:T(8,128)} %shard_map.86, f32[16,2048]{1,0:T(8,128)S(1)} %copy-done), kind=kLoop, calls=%fused_computation.1 | loop fusion | flops 98304 | bytes 524288 | tf_op jit(solution)/shard_map/mul | solution.py:454
Async XLA Ops:
  35.5 84.0 %copy-start = (f32[16,2048]{1,0:T(8,128)S(1)}, f32[16,2048]{1,0:T(8,128)}, u32[]{:S(2)}) copy-start(f32[16,2048]{1,0:T(8,128)} %latent_ref.1) | copy-start | bytes 393220

commit v2 on v1

--- a/solution.py
+++ b/solution.py
@@ -110,22 +110,24 @@
 
 PACK = 16
 BLOCKS = PACK // CAP
+HALVES = 2
 MESH = pl.DeviceIdType.MESH
 
 
 def kernel(
     sizes,
-    latent_ref, te_ref, gain_ref, router_hbm, up_hbm, down_hbm, routes_ref,
+    latent_ref, te_ref, gain_ref, router_ref, up_hbm, down_hbm, routes_ref,
     out_ref,
     up_v, down_v, router_v, base, state, total,
     take_first, take_second, spread, unpack, pack,
     dsend, xbuf, ybuf, yrecv, zsend, rbuf,
-    w_sem, router_sem, d_send, d_recv, f_send, f_recv, y_send, y_recv, r_send, r_recv,
+    w_sem, d_send, d_recv, n_send, n_recv, f_send, f_recv, y_send, y_recv, r_send, r_recv,
 ):
     nz, nc, layers, per_core, toks, width = sizes
     cols = width // BLOCKS
     srcs = 2 * nz * nc
     half = nz * nc
+    part = width // HALVES
     z = lax.axis_index("expert")
     x = lax.axis_index("dp")
     c = lax.axis_index("mp")
@@ -139,22 +141,30 @@
             ),
         )
 
-    router_copy = pltpu.make_async_copy(router_hbm, router_v, router_sem)
     for layer in range(layers):
         for j in range(per_core):
             for copy in weight_copies(layer, j):
                 copy.start()
-        if layer == 0:
-            router_copy.start()
+
+    def across(place, offset):
+        bit = 1
+        while bit <= offset:
+            if offset & bit:
+                place = place + bit - 2 * bit * lax.rem(lax.div(place, bit), 2)
+            bit *= 2
+        return place
 
     barrier = pltpu.get_barrier_semaphore()
-    others = [(dz, dc) for dz in range(nz) for dc in range(nc) if (dz, dc) != (0, 0)]
-    for dz, dc in others:
-        pl.semaphore_signal(
-            barrier, inc=1, device_id={"expert": lax.rem(z + dz, nz), "mp": lax.rem(c + dc, nc)},
-            device_id_type=MESH,
-        )
-    pl.semaphore_signal(barrier, inc=1, device_id={"dp": 1 - x}, device_id_type=MESH)
+    others = [(dz, dc) for dz in range(nz - 1, -1, -1) for dc in range(nc) if (dz, dc) != (0, 0)]
+    for side in (x, 1 - x):
+        for dz, dc in others + [(0, 0)]:
+            if side is x and (dz, dc) == (0, 0):
+                continue
+            pl.semaphore_signal(
+                barrier, inc=1,
+                device_id={"expert": across(z, dz), "dp": side, "mp": across(c, dc)},
+                device_id_type=MESH,
+            )
 
     def places(rows, lanes, target):
         lane = lax.broadcasted_iota(jnp.int32, (rows, lanes), 1)
@@ -173,9 +183,18 @@
     ).astype(jnp.bfloat16)
     experts = nz * nc * per_core
 
+    def columns(chosen):
+        same = lax.broadcasted_iota(jnp.int32, (toks, toks), 0) == lax.broadcasted_iota(
+            jnp.int32, (toks, toks), 1
+        )
+        chosen = chosen.astype(jnp.float32)
+        return [
+            jnp.sum(jnp.where(same, chosen[n:n + 1, :], 0.0), axis=1, keepdims=True).astype(jnp.int32)
+            for n in range(2)
+        ]
+
     def route(p, carry):
-        chosen = routes_ref[p // layers, p % layers]
-        first, second = chosen[:, 0:1], chosen[:, 1:2]
+        first, second = columns(routes_ref[p // layers, p % layers])
         lane = lax.broadcasted_iota(jnp.int32, (toks, 128), 1)
         one = jnp.where(lane == first, 1.0, 0.0)
         two = jnp.where(lane == second, 1.0, 0.0)
@@ -198,12 +217,15 @@
         return carry
 
     lax.fori_loop(0, 2 * layers, route, 0)
+    for layer in range(layers):
+        high = router_ref[layer].astype(jnp.bfloat16)
+        router_v[layer, :experts] = high
+        router_v[layer, experts:] = (router_ref[layer] - high.astype(jnp.float32)).astype(jnp.bfloat16)
     base[...] = latent_ref[...]
-    pl.semaphore_wait(barrier, len(others) + 1)
-    router_copy.wait()
+    pl.semaphore_wait(barrier, srcs - 1)
 
     def dispatch_copy(j, dz, dc, src_z, src_c):
-        to_z, to_c = lax.rem(src_z + dz, nz), lax.rem(src_c + dc, nc)
+        to_z, to_c = across(src_z, dz), across(src_c, dc)
         expert = (to_z * nc + to_c) * per_core + j
         return pltpu.make_async_remote_copy(
             src_ref=dsend.at[pl.ds(pl.multiple_of(expert * PACK, PACK), PACK)],
@@ -216,8 +238,25 @@
             device_id_type=MESH,
         )
 
+    def near_copy(j, dz, dc, src_x, src_z, src_c):
+        to_z, to_c = across(src_z, dz), across(src_c, dc)
+        expert = (to_z * nc + to_c) * per_core + j
+        return pltpu.make_async_remote_copy(
+            src_ref=dsend.at[pl.ds(pl.multiple_of(expert * PACK, PACK), PACK)],
+            dst_ref=xbuf.at[
+                j, pl.ds(pl.multiple_of(((src_x * nz + src_z) * nc + src_c) * PACK, PACK), PACK)
+            ],
+            send_sem=n_send.at[j, dz, dc],
+            recv_sem=n_recv.at[j, dz, dc],
+            device_id={"expert": to_z, "dp": 1 - src_x, "mp": to_c},
+            device_id_type=MESH,
+        )
+
+    near = [(dz, dc) for dz in range(min(2, nz)) for dc in range(nc)]
+    far = list(range(2, nz))
+
     def forward_copy(j, dz, side):
-        src_z = lax.rem(z + nz - dz, nz)
+        src_z = across(z, dz)
         rows = pl.ds(pl.multiple_of((side * nz + src_z) * nc * PACK, nc * PACK), nc * PACK)
         return pltpu.make_async_remote_copy(
             src_ref=xbuf.at[j, rows],
@@ -228,18 +267,18 @@
             device_id_type=MESH,
         )
 
-    def result_copy(j):
+    def result_copy(j, h):
         return pltpu.make_async_remote_copy(
-            src_ref=ybuf.at[j, 1 - x],
-            dst_ref=yrecv.at[j],
-            send_sem=y_send.at[j],
-            recv_sem=y_recv.at[j],
+            src_ref=ybuf.at[j, h, 1 - x],
+            dst_ref=yrecv.at[j, h],
+            send_sem=y_send.at[j, h],
+            recv_sem=y_recv.at[j, h],
             device_id={"dp": 1 - x},
             device_id_type=MESH,
         )
 
     def return_copy(j, dz, dc, src_z, src_c):
-        to_z, to_c = lax.rem(src_z + dz, nz), lax.rem(src_c + dc, nc)
+        to_z, to_c = across(src_z, dz), across(src_c, dc)
         expert = (src_z * nc + src_c) * per_core + j
         return pltpu.make_async_remote_copy(
             src_ref=zsend.at[j, pl.ds(pl.multiple_of((to_z * nc + to_c) * PACK, PACK), PACK)],
@@ -251,7 +290,7 @@
         )
 
     def came_from(dz, dc):
-        return lax.rem(z + nz - dz, nz), lax.rem(c + nc - dc, nc)
+        return across(z, dz), across(c, dc)
 
     def step(p, carry):
         layer = lax.rem(p, layers)
@@ -275,32 +314,39 @@
         for j in range(per_core):
             for dz, dc in others:
                 dispatch_copy(j, dz, dc, z, c).start()
+            for dz, dc in reversed(near):
+                near_copy(j, dz, dc, x, z, c).start()
         for j in range(per_core):
             expert = (z * nc + c) * per_core + j
             xbuf[j, pl.ds(pl.multiple_of(((x * nz + z) * nc + c) * PACK, PACK), PACK)] = dsend[
                 pl.ds(pl.multiple_of(expert * PACK, PACK), PACK)
             ]
 
-        logits = jnp.dot(
-            scaled, router_v[layer], precision=lax.Precision.HIGHEST,
+        low = (scaled - normed.astype(jnp.float32)).astype(jnp.bfloat16)
+        parts = lax.dot_general(
+            jnp.concatenate([normed, low], axis=0), router_v[layer], (((1,), (1,)), ((), ())),
             preferred_element_type=jnp.float32,
         )
-        chosen = routes_ref[evaluation, layer]
-        lane = lax.broadcasted_iota(jnp.int32, logits.shape, 1)
-        of_first = jnp.sum(jnp.where(lane == chosen[:, 0:1], logits, 0.0), axis=1, keepdims=True)
-        of_second = jnp.sum(jnp.where(lane == chosen[:, 1:2], logits, 0.0), axis=1, keepdims=True)
+        logits = parts[:toks] + parts[toks:]
+        first, second = columns(routes_ref[evaluation, layer])
+        lane = lax.rem(lax.broadcasted_iota(jnp.int32, logits.shape, 1), experts)
+        of_first = jnp.sum(jnp.where(lane == first, logits, 0.0), axis=1, keepdims=True)
+        of_second = jnp.sum(jnp.where(lane == second, logits, 0.0), axis=1, keepdims=True)
         mix0 = jax.nn.sigmoid(of_first - of_second)
         mix1 = 1.0 - mix0
 
         for j in range(per_core):
-            for dz in range(nz):
+            for dz in far:
                 for dc in range(nc):
-                    if (dz, dc) != (0, 0):
-                        dispatch_copy(j, dz, dc, *came_from(dz, dc)).wait_recv()
+                    dispatch_copy(j, dz, dc, *came_from(dz, dc)).wait_recv()
                 forward_copy(j, dz, x).start()
 
         for j in range(per_core):
-            for dz in range(nz):
+            for dz, dc in near:
+                if (dz, dc) != (0, 0):
+                    dispatch_copy(j, dz, dc, *came_from(dz, dc)).wait_recv()
+                near_copy(j, dz, dc, 1 - x, *came_from(dz, dc)).wait_recv()
+            for dz in far:
                 forward_copy(j, dz, 1 - x).wait_recv()
 
             @pl.when(evaluation == 0)
@@ -311,34 +357,34 @@
             rows = jnp.dot(
                 unpack[...], xbuf[j], preferred_element_type=jnp.float32
             ).astype(jnp.bfloat16)
-            acc = jnp.dot(
-                rows[:per_block], up_v[layer, j, :cols, :], preferred_element_type=jnp.float32
+            wide = jnp.concatenate(
+                [rows[b * per_block:(b + 1) * per_block] for b in range(BLOCKS)], axis=1
             )
-            for b in range(1, BLOCKS):
-                acc += jnp.dot(
-                    rows[b * per_block:(b + 1) * per_block],
-                    up_v[layer, j, b * cols:(b + 1) * cols, :],
+            acc = lax.dot_general(
+                wide, up_v[layer, j], (((1,), (1,)), ((), ())), preferred_element_type=jnp.float32
+            )
+            hidden = jax.nn.gelu(acc, approximate=True).astype(jnp.bfloat16)
+            for h in range(HALVES):
+                out = jnp.dot(
+                    hidden, down_v[layer, j, :, h * part:(h + 1) * part],
                     preferred_element_type=jnp.float32,
-                )
-            hidden = jax.nn.gelu(acc, approximate=True).astype(jnp.bfloat16)
-            out = jnp.dot(
-                hidden, down_v[layer, j], preferred_element_type=jnp.float32
-            ).astype(jnp.bfloat16)
-            ybuf[j, 0] = out[:per_block // 2]
-            ybuf[j, 1] = out[per_block // 2:]
-            result_copy(j).start()
-
-        for j in range(per_core):
-            for dz in range(nz):
+                ).astype(jnp.bfloat16)
+                ybuf[j, h, 0] = out[:per_block // 2]
+                ybuf[j, h, 1] = out[per_block // 2:]
+                result_copy(j, h).start()
+
+        for j in range(per_core):
+            for dz in far:
                 forward_copy(j, dz, x).wait_send()
         for j in range(per_core):
-            result_copy(j).wait_recv()
-            summed = (
-                ybuf[j, x].astype(jnp.float32) + yrecv[j].astype(jnp.float32)
-            ).astype(jnp.bfloat16)
-            tall = jnp.concatenate(
-                [summed[:, b * cols:(b + 1) * cols] for b in range(BLOCKS)], axis=0
-            )
+            pieces = []
+            for h in range(HALVES):
+                result_copy(j, h).wait_recv()
+                summed = (
+                    ybuf[j, h, x].astype(jnp.float32) + yrecv[j, h].astype(jnp.float32)
+                ).astype(jnp.bfloat16)
+                pieces += [summed[:, b * cols:(b + 1) * cols] for b in range(BLOCKS // HALVES)]
+            tall = jnp.concatenate(pieces, axis=0)
             zsend[j] = jnp.dot(
                 pack[...], tall, preferred_element_type=jnp.float32
             ).astype(jnp.bfloat16)
@@ -350,9 +396,12 @@
             ]
 
         for j in range(per_core):
-            result_copy(j).wait_send()
+            for h in range(HALVES):
+                result_copy(j, h).wait_send()
             for dz, dc in others:
                 dispatch_copy(j, dz, dc, z, c).wait_send()
+            for dz, dc in near:
+                near_copy(j, dz, dc, x, z, c).wait_send()
         for j in range(per_core):
             for dz, dc in others:
                 return_copy(j, dz, dc, *came_from(dz, dc)).wait_recv()
@@ -389,6 +438,8 @@
         and local_experts % nc == 0
         and local_experts * nz == experts
         and local_experts // nc <= 2
+        and nz & (nz - 1) == 0
+        and nc & (nc - 1) == 0
         and toks % 16 == 0
         and width % (BLOCKS * 128) == 0
         and hidden % 16 == 0
@@ -411,12 +462,12 @@
     total = pl.pallas_call(
         functools.partial(kernel, (nz, nc, layers, per_core, toks, width)),
         out_shape=jax.ShapeDtypeStruct((toks, width), f32),
-        in_specs=[vmem, vmem, vmem, hbm, hbm, hbm, vmem],
+        in_specs=[vmem, vmem, vmem, vmem, hbm, hbm, vmem],
         out_specs=vmem,
         scratch_shapes=[
-            pltpu.VMEM((layers, per_core, width, hidden), bf16),
             pltpu.VMEM((layers, per_core, hidden, width), bf16),
-            pltpu.VMEM((layers, width, experts), f32),
+            pltpu.VMEM((layers, per_core, hidden, width), bf16),
+            pltpu.VMEM((layers, 2 * experts, width), bf16),
             pltpu.VMEM((toks, width), f32),
             pltpu.VMEM((toks, width), f32),
             pltpu.VMEM((toks, width), f32),
@@ -427,18 +478,19 @@
             pltpu.VMEM((half * PACK, half * PACK), bf16),
             pltpu.VMEM((experts * PACK, cols), bf16),
             pltpu.VMEM((per_core, srcs * PACK, cols), bf16),
-            pltpu.VMEM((per_core, 2, half * CAP, width), bf16),
-            pltpu.VMEM((per_core, half * CAP, width), bf16),
+            pltpu.VMEM((per_core, HALVES, 2, half * CAP, width // HALVES), bf16),
+            pltpu.VMEM((per_core, HALVES, half * CAP, width // HALVES), bf16),
             pltpu.VMEM((per_core, half * PACK, cols), bf16),
             pltpu.VMEM((experts * PACK, cols), bf16),
             dma((layers, per_core, 2)),
-            dma,
+            dma((per_core, nz, nc)),
+            dma((per_core, nz, nc)),
             dma((per_core, nz, nc)),
             dma((per_core, nz, nc)),
             dma((per_core, nz)),
             dma((per_core, nz)),
-            dma((per_core,)),
-            dma((per_core,)),
+            dma((per_core, HALVES)),
+            dma((per_core, HALVES)),
             dma((per_core, nz, nc)),
             dma((per_core, nz, nc)),
         ],
@@ -450,7 +502,10 @@
             bytes_accessed=layers * per_core * width * hidden * 4,
             transcendentals=0,
         ),
-    )(latent, time_embedding.reshape(1, width), norm_gain, router, up_proj, down_proj, routes)
+    )(
+        latent, time_embedding.reshape(1, width), norm_gain, jnp.swapaxes(router, 1, 2),
+        jnp.swapaxes(up_proj, 2, 3), down_proj, jnp.swapaxes(routes, 2, 3),
+    )
     mean_velocity = 0.5 * total
     return (latent + step_size * mean_velocity, mean_velocity)
 

time: 122 us -> 82.1 us (0.67)
  local copies, waits for them, and re-layouts: 34.9 us -> 0.01 us
  Pallas kernels: 84 us -> 79.6 us
    unnamed x5 -> x2, local copies, waits for them, and re-layouts: 34.9 us -> 0.01 us
    pallas_call x1, Pallas kernels: 84 us -> 79.6 us  [per_device(): pl.pallas_call(functools.partial(kernel, (nz, nc, layers, per_core, toks,...]
where the time goes in v2:
time: 82.1 us; the launch traced here: 81.9 us
  Pallas kernels  79.6 us (97%)
  other arithmetic  1.62 us (2%)
    pallas_call x1, Pallas kernels, per_device(): pl.pallas_call(functools.partial(kernel, (nz, nc, layers, per_core, toks,...  79.6 us

profile of v2, /device:TPU:0, one launch (start us, length us, event | category | flops | bytes accessed | tf_op | source)
XLA Modules:
  0.0 81.9 jit_solution(1329827370903359124)
XLA Ops:
  0.6 0.0 copy-start
  0.6 79.6 %shard_map.86 = f32[16,2048]{1,0:T(8,128)} custom-call(f32[16,2048]{1,0:T(8,128)} %latent_ref.1, f32[1,2048]{1,0:T(1,128)} %bitcast.6, f32[2,2048]{1,0:T(2,128)} %gain_ref.1, f32[2,16,2048]{2,1,0:T(8,128)} %bitcast.5, bf16[2,4,704,2048]{3,2,1,0:T(8,128)(2,1)} %bitcast.4, bf16[2,4,704,2048]{3,2,1,0:T(8,128)(2,1)} %down_hbm.1, s32[2,2,2,16]{3,2,1,0:T(2,128)} %bitcast.7), custom_call_target="tpu_custom_call" | custom-call | flops 1476395008 | bytes 23068672 | tf_op jit(solution)/shard_map/pallas_call | solution.py:462
  80.3 0.0 copy-done
  80.3 1.6 %broadcast_multiply_fusion = (f32[16,2048]{1,0:T(8,128)}, f32[16,2048]{1,0:T(8,128)}) fusion(f32[16,2048]{1,0:T(8,128)} %shard_map.86, f32[16,2048]{1,0:T(8,128)S(1)} %copy-done), kind=kLoop, calls=%fused_computation.1 | loop fusion | flops 98304 | bytes 524288 | tf_op jit(solution)/shard_map/mul | solution.py:509
Async XLA Ops:
  0.6 79.6 %copy-start = (f32[16,2048]{1,0:T(8,128)S(1)}, f32[16,2048]{1,0:T(8,128)}, u32[]{:S(2)}) copy-start(f32[16,2048]{1,0:T(8,128)} %latent_ref.1) | copy-start | bytes 393220

commit v3 on v2

--- a/solution.py
+++ b/solution.py
@@ -110,7 +110,6 @@
 
 PACK = 16
 BLOCKS = PACK // CAP
-HALVES = 2
 MESH = pl.DeviceIdType.MESH
 
 
@@ -120,14 +119,14 @@
     out_ref,
     up_v, down_v, router_v, base, state, total,
     take_first, take_second, spread, unpack, pack,
-    dsend, xbuf, ybuf, yrecv, zsend, rbuf,
+    dsend, xbuf, pbuf, yrecv, zsend, rbuf,
     w_sem, d_send, d_recv, n_send, n_recv, f_send, f_recv, y_send, y_recv, r_send, r_recv,
+    b_send, b_recv,
 ):
     nz, nc, layers, per_core, toks, width = sizes
     cols = width // BLOCKS
     srcs = 2 * nz * nc
     half = nz * nc
-    part = width // HALVES
     z = lax.axis_index("expert")
     x = lax.axis_index("dp")
     c = lax.axis_index("mp")
@@ -154,6 +153,7 @@
             bit *= 2
         return place
 
+    rbuf[...] = jnp.zeros_like(rbuf)
     barrier = pltpu.get_barrier_semaphore()
     others = [(dz, dc) for dz in range(nz - 1, -1, -1) for dc in range(nc) if (dz, dc) != (0, 0)]
     for side in (x, 1 - x):
@@ -176,10 +176,8 @@
     unpack[...] = places(
         rows_in, rows_in, (i % per_block) // CAP * PACK + i // per_block * CAP + i % CAP
     ).astype(jnp.bfloat16)
-    back = half * PACK
-    i = lax.broadcasted_iota(jnp.int32, (back, 1), 0)
     pack[...] = places(
-        back, back, (i % PACK) // CAP * (half * CAP) + i // PACK * CAP + i % CAP
+        rows_in, rows_in, (i % PACK) // CAP * per_block + i // PACK * CAP + i % CAP
     ).astype(jnp.bfloat16)
     experts = nz * nc * per_core
 
@@ -224,70 +222,82 @@
     base[...] = latent_ref[...]
     pl.semaphore_wait(barrier, srcs - 1)
 
+    near = [
+        (dx, dz, dc) for dx in (1, 0) for dz in (1, 0) for dc in range(nc) if (dx, dz, dc) != (0, 0, 0)
+    ]
+    far = [(dz, dc) for dz in range(2, nz) for dc in range(nc)]
+    far_count = (nz - 2) * nc
+
+    def far_start(place):
+        return 2 - 2 * lax.div(place, 2)
+
     def dispatch_copy(j, dz, dc, src_z, src_c):
         to_z, to_c = across(src_z, dz), across(src_c, dc)
-        expert = (to_z * nc + to_c) * per_core + j
         return pltpu.make_async_remote_copy(
-            src_ref=dsend.at[pl.ds(pl.multiple_of(expert * PACK, PACK), PACK)],
-            dst_ref=xbuf.at[
-                j, pl.ds(pl.multiple_of(((x * nz + src_z) * nc + src_c) * PACK, PACK), PACK)
-            ],
+            src_ref=dsend.at[to_z * nc + to_c, j],
+            dst_ref=xbuf.at[(x * nz + src_z) * nc + src_c, j],
             send_sem=d_send.at[j, dz, dc],
             recv_sem=d_recv.at[j, dz, dc],
             device_id={"expert": to_z, "mp": to_c},
             device_id_type=MESH,
         )
 
-    def near_copy(j, dz, dc, src_x, src_z, src_c):
-        to_z, to_c = across(src_z, dz), across(src_c, dc)
-        expert = (to_z * nc + to_c) * per_core + j
+    def near_copy(dx, dz, dc, src_x, src_z, src_c):
+        to_x, to_z, to_c = across(src_x, dx), across(src_z, dz), across(src_c, dc)
         return pltpu.make_async_remote_copy(
-            src_ref=dsend.at[pl.ds(pl.multiple_of(expert * PACK, PACK), PACK)],
-            dst_ref=xbuf.at[
-                j, pl.ds(pl.multiple_of(((src_x * nz + src_z) * nc + src_c) * PACK, PACK), PACK)
-            ],
-            send_sem=n_send.at[j, dz, dc],
-            recv_sem=n_recv.at[j, dz, dc],
-            device_id={"expert": to_z, "dp": 1 - src_x, "mp": to_c},
+            src_ref=dsend.at[to_z * nc + to_c],
+            dst_ref=xbuf.at[(src_x * nz + src_z) * nc + src_c],
+            send_sem=n_send.at[dx, dz, dc],
+            recv_sem=n_recv.at[dx, dz, dc],
+            device_id={"expert": to_z, "dp": to_x, "mp": to_c},
             device_id_type=MESH,
         )
 
-    near = [(dz, dc) for dz in range(min(2, nz)) for dc in range(nc)]
-    far = list(range(2, nz))
-
     def forward_copy(j, dz, side):
-        src_z = across(z, dz)
-        rows = pl.ds(pl.multiple_of((side * nz + src_z) * nc * PACK, nc * PACK), nc * PACK)
+        rows = pl.ds((side * nz + across(z, dz)) * nc, nc)
         return pltpu.make_async_remote_copy(
-            src_ref=xbuf.at[j, rows],
-            dst_ref=xbuf.at[j, rows],
+            src_ref=xbuf.at[rows, j],
+            dst_ref=xbuf.at[rows, j],
             send_sem=f_send.at[j, dz],
             recv_sem=f_recv.at[j, dz],
             device_id={"dp": 1 - x},
             device_id_type=MESH,
         )
 
-    def result_copy(j, h):
+    def result_copy(j):
         return pltpu.make_async_remote_copy(
-            src_ref=ybuf.at[j, h, 1 - x],
-            dst_ref=yrecv.at[j, h],
-            send_sem=y_send.at[j, h],
-            recv_sem=y_recv.at[j, h],
+            src_ref=pbuf.at[pl.ds(((1 - x) * nz + far_start(z)) * nc, far_count), j],
+            dst_ref=yrecv.at[j],
+            send_sem=y_send.at[j],
+            recv_sem=y_recv.at[j],
             device_id={"dp": 1 - x},
             device_id_type=MESH,
         )
 
     def return_copy(j, dz, dc, src_z, src_c):
         to_z, to_c = across(src_z, dz), across(src_c, dc)
-        expert = (src_z * nc + src_c) * per_core + j
         return pltpu.make_async_remote_copy(
-            src_ref=zsend.at[j, pl.ds(pl.multiple_of((to_z * nc + to_c) * PACK, PACK), PACK)],
-            dst_ref=rbuf.at[pl.ds(pl.multiple_of(expert * PACK, PACK), PACK)],
+            src_ref=zsend.at[j, (to_z - far_start(src_z)) * nc + to_c],
+            dst_ref=rbuf.at[0, src_z * nc + src_c, j],
             send_sem=r_send.at[j, dz, dc],
             recv_sem=r_recv.at[j, dz, dc],
             device_id={"expert": to_z, "mp": to_c},
             device_id_type=MESH,
         )
+
+    def back_copy(dx, dz, dc, src_x, src_z, src_c):
+        to_x, to_z, to_c = across(src_x, dx), across(src_z, dz), across(src_c, dc)
+        return pltpu.make_async_remote_copy(
+            src_ref=pbuf.at[(to_x * nz + to_z) * nc + to_c],
+            dst_ref=rbuf.at[dx, src_z * nc + src_c],
+            send_sem=b_send.at[dx, dz, dc],
+            recv_sem=b_recv.at[dx, dz, dc],
+            device_id={"expert": to_z, "dp": to_x, "mp": to_c},
+            device_id_type=MESH,
+        )
+
+    def near_from(dx, dz, dc):
+        return across(x, dx), across(z, dz), across(c, dc)
 
     def came_from(dz, dc):
         return across(z, dz), across(c, dc)
@@ -310,17 +320,13 @@
         )
         dsend[...] = jnp.dot(
             spread[p], stacked, preferred_element_type=jnp.float32
-        ).astype(jnp.bfloat16)
-        for j in range(per_core):
-            for dz, dc in others:
+        ).astype(jnp.bfloat16).reshape(dsend.shape)
+        for j in range(per_core):
+            for dz, dc in far:
                 dispatch_copy(j, dz, dc, z, c).start()
-            for dz, dc in reversed(near):
-                near_copy(j, dz, dc, x, z, c).start()
-        for j in range(per_core):
-            expert = (z * nc + c) * per_core + j
-            xbuf[j, pl.ds(pl.multiple_of(((x * nz + z) * nc + c) * PACK, PACK), PACK)] = dsend[
-                pl.ds(pl.multiple_of(expert * PACK, PACK), PACK)
-            ]
+        for offset in near:
+            near_copy(*offset, x, z, c).start()
+        xbuf[(x * nz + z) * nc + c] = dsend[z * nc + c]
 
         low = (scaled - normed.astype(jnp.float32)).astype(jnp.bfloat16)
         parts = lax.dot_general(
@@ -336,17 +342,15 @@
         mix1 = 1.0 - mix0
 
         for j in range(per_core):
-            for dz in far:
+            for dz in range(2, nz):
                 for dc in range(nc):
                     dispatch_copy(j, dz, dc, *came_from(dz, dc)).wait_recv()
                 forward_copy(j, dz, x).start()
-
-        for j in range(per_core):
-            for dz, dc in near:
-                if (dz, dc) != (0, 0):
-                    dispatch_copy(j, dz, dc, *came_from(dz, dc)).wait_recv()
-                near_copy(j, dz, dc, 1 - x, *came_from(dz, dc)).wait_recv()
-            for dz in far:
+        for offset in near:
+            near_copy(*offset, *near_from(*offset)).wait_recv()
+
+        for j in range(per_core):
+            for dz in range(2, nz):
                 forward_copy(j, dz, 1 - x).wait_recv()
 
             @pl.when(evaluation == 0)
@@ -355,7 +359,7 @@
                     copy.wait()
 
             rows = jnp.dot(
-                unpack[...], xbuf[j], preferred_element_type=jnp.float32
+                unpack[...], xbuf[:, j].reshape(rows_in, cols), preferred_element_type=jnp.float32
             ).astype(jnp.bfloat16)
             wide = jnp.concatenate(
                 [rows[b * per_block:(b + 1) * per_block] for b in range(BLOCKS)], axis=1
@@ -364,56 +368,60 @@
                 wide, up_v[layer, j], (((1,), (1,)), ((), ())), preferred_element_type=jnp.float32
             )
             hidden = jax.nn.gelu(acc, approximate=True).astype(jnp.bfloat16)
-            for h in range(HALVES):
-                out = jnp.dot(
-                    hidden, down_v[layer, j, :, h * part:(h + 1) * part],
-                    preferred_element_type=jnp.float32,
-                ).astype(jnp.bfloat16)
-                ybuf[j, h, 0] = out[:per_block // 2]
-                ybuf[j, h, 1] = out[per_block // 2:]
-                result_copy(j, h).start()
-
-        for j in range(per_core):
-            for dz in far:
+            out = jnp.dot(
+                hidden, down_v[layer, j], preferred_element_type=jnp.float32
+            ).astype(jnp.bfloat16)
+            tall = jnp.concatenate(
+                [out[:, b * cols:(b + 1) * cols] for b in range(BLOCKS)], axis=0
+            )
+            pbuf[:, j] = jnp.dot(
+                pack[...], tall, preferred_element_type=jnp.float32
+            ).astype(jnp.bfloat16).reshape(srcs, PACK, cols)
+            result_copy(j).start()
+
+        for j in range(per_core):
+            for dz in range(2, nz):
                 forward_copy(j, dz, x).wait_send()
-        for j in range(per_core):
-            pieces = []
-            for h in range(HALVES):
-                result_copy(j, h).wait_recv()
-                summed = (
-                    ybuf[j, h, x].astype(jnp.float32) + yrecv[j, h].astype(jnp.float32)
-                ).astype(jnp.bfloat16)
-                pieces += [summed[:, b * cols:(b + 1) * cols] for b in range(BLOCKS // HALVES)]
-            tall = jnp.concatenate(pieces, axis=0)
-            zsend[j] = jnp.dot(
-                pack[...], tall, preferred_element_type=jnp.float32
+        for offset in near:
+            back_copy(*offset, x, z, c).start()
+        rbuf[0, z * nc + c] = pbuf[(x * nz + z) * nc + c]
+        for j in range(per_core):
+            result_copy(j).wait_recv()
+            zsend[j] = (
+                pbuf[pl.ds((x * nz + far_start(z)) * nc, far_count), j].astype(jnp.float32)
+                + yrecv[j].astype(jnp.float32)
             ).astype(jnp.bfloat16)
-            for dz, dc in others:
+            for dz, dc in far:
                 return_copy(j, dz, dc, z, c).start()
-            expert = (z * nc + c) * per_core + j
-            rbuf[pl.ds(pl.multiple_of(expert * PACK, PACK), PACK)] = zsend[
-                j, pl.ds(pl.multiple_of((z * nc + c) * PACK, PACK), PACK)
-            ]
-
-        for j in range(per_core):
-            for h in range(HALVES):
-                result_copy(j, h).wait_send()
-            for dz, dc in others:
+
+        for j in range(per_core):
+            result_copy(j).wait_send()
+            for dz, dc in far:
                 dispatch_copy(j, dz, dc, z, c).wait_send()
-            for dz, dc in near:
-                near_copy(j, dz, dc, x, z, c).wait_send()
-        for j in range(per_core):
-            for dz, dc in others:
+        for offset in near:
+            near_copy(*offset, x, z, c).wait_send()
+            back_copy(*offset, x, z, c).wait_send()
+        for offset in near:
+            back_copy(*offset, *near_from(*offset)).wait_recv()
+        for j in range(per_core):
+            for dz, dc in far:
                 return_copy(j, dz, dc, *came_from(dz, dc)).wait_recv()
-        returned = rbuf[...]
-        g0 = jnp.dot(take_first[p], returned, preferred_element_type=jnp.float32)
-        g1 = jnp.dot(take_second[p], returned, preferred_element_type=jnp.float32)
+        mine = rbuf[0].reshape(experts * PACK, cols)
+        other = rbuf[1].reshape(experts * PACK, cols)
+
+        def taken(take):
+            both = jnp.dot(take, mine, preferred_element_type=jnp.float32) + jnp.dot(
+                take, other, preferred_element_type=jnp.float32
+            )
+            return both.astype(jnp.bfloat16).astype(jnp.float32)
+
+        g0, g1 = taken(take_first[p]), taken(take_second[p])
         for b in range(BLOCKS):
             r = slice(b * toks, (b + 1) * toks)
             w = slice(b * cols, (b + 1) * cols)
             state[:, w] = old[:, w] + (mix0 * g0[r] + mix1 * g1[r])
         for j in range(per_core):
-            for dz, dc in others:
+            for dz, dc in far:
                 return_copy(j, dz, dc, z, c).wait_send()
 
         @pl.when(p == layers - 1)
@@ -438,7 +446,7 @@
         and local_experts % nc == 0
         and local_experts * nz == experts
         and local_experts // nc <= 2
-        and nz & (nz - 1) == 0
+        and nz == 4
         and nc & (nc - 1) == 0
         and toks % 16 == 0
         and width % (BLOCKS * 128) == 0
@@ -475,24 +483,26 @@
             pltpu.VMEM((2 * layers, BLOCKS * toks, experts * PACK), bf16),
             pltpu.VMEM((2 * layers, experts * PACK, BLOCKS * toks), bf16),
             pltpu.VMEM((srcs * PACK, srcs * PACK), bf16),
-            pltpu.VMEM((half * PACK, half * PACK), bf16),
-            pltpu.VMEM((experts * PACK, cols), bf16),
-            pltpu.VMEM((per_core, srcs * PACK, cols), bf16),
-            pltpu.VMEM((per_core, HALVES, 2, half * CAP, width // HALVES), bf16),
-            pltpu.VMEM((per_core, HALVES, half * CAP, width // HALVES), bf16),
-            pltpu.VMEM((per_core, half * PACK, cols), bf16),
-            pltpu.VMEM((experts * PACK, cols), bf16),
+            pltpu.VMEM((srcs * PACK, srcs * PACK), bf16),
+            pltpu.VMEM((half, per_core, PACK, cols), bf16),
+            pltpu.VMEM((srcs, per_core, PACK, cols), bf16),
+            pltpu.VMEM((srcs, per_core, PACK, cols), bf16),
+            pltpu.VMEM((per_core, (nz - 2) * nc, PACK, cols), bf16),
+            pltpu.VMEM((per_core, (nz - 2) * nc, PACK, cols), bf16),
+            pltpu.VMEM((2, half, per_core, PACK, cols), bf16),
             dma((layers, per_core, 2)),
             dma((per_core, nz, nc)),
             dma((per_core, nz, nc)),
+            dma((2, 2, nc)),
+            dma((2, 2, nc)),
+            dma((per_core, nz)),
+            dma((per_core, nz)),
+            dma((per_core,)),
+            dma((per_core,)),
             dma((per_core, nz, nc)),
             dma((per_core, nz, nc)),
-            dma((per_core, nz)),
-            dma((per_core, nz)),
-            dma((per_core, HALVES)),
-            dma((per_core, HALVES)),
-            dma((per_core, nz, nc)),
-            dma((per_core, nz, nc)),
+            dma((2, 2, nc)),
+            dma((2, 2, nc)),
         ],
         compiler_params=pltpu.CompilerParams(
             collective_id=0, has_side_effects=True, vmem_limit_bytes=56 * 1024 * 1024

time: 82.1 us -> 84.9 us (1.034)
  Pallas kernels: 79.6 us -> 82.5 us
    pallas_call x1, Pallas kernels: 79.6 us -> 82.5 us  [per_device(): pl.pallas_call(functools.partial(kernel, (nz, nc, layers, per_core, toks,...]
where the time goes in v3:
time: 84.9 us; the launch traced here: 84.8 us
  Pallas kernels  82.5 us (97%)
  other arithmetic  1.62 us (2%)
    pallas_call x1, Pallas kernels, per_device(): pl.pallas_call(functools.partial(kernel, (nz, nc, layers, per_core, toks,...  82.5 us

profile of v3, /device:TPU:0, one launch (start us, length us, event | category | flops | bytes accessed | tf_op | source)
XLA Modules:
  0.0 84.8 jit_solution(3961784969134702548)
XLA Ops:
  0.6 0.0 copy-start
  0.6 82.5 %shard_map.86 = f32[16,2048]{1,0:T(8,128)} custom-call(f32[16,2048]{1,0:T(8,128)} %latent_ref.1, f32[1,2048]{1,0:T(1,128)} %bitcast.6, f32[2,2048]{1,0:T(2,128)} %gain_ref.1, f32[2,16,2048]{2,1,0:T(8,128)} %bitcast.5, bf16[2,4,704,2048]{3,2,1,0:T(8,128)(2,1)} %bitcast.4, bf16[2,4,704,2048]{3,2,1,0:T(8,128)(2,1)} %down_hbm.1, s32[2,2,2,16]{3,2,1,0:T(2,128)} %bitcast.7), custom_call_target="tpu_custom_call" | custom-call | flops 1476395008 | bytes 23068672 | tf_op jit(solution)/shard_map/pallas_call | solution.py:470
  83.1 0.0 copy-done
  83.1 1.6 %broadcast_multiply_fusion = (f32[16,2048]{1,0:T(8,128)}, f32[16,2048]{1,0:T(8,128)}) fusion(f32[16,2048]{1,0:T(8,128)} %shard_map.86, f32[16,2048]{1,0:T(8,128)S(1)} %copy-done), kind=kLoop, calls=%fused_computation.1 | loop fusion | flops 98304 | bytes 524288 | tf_op jit(solution)/shard_map/mul | solution.py:519
Async XLA Ops:
  0.6 82.5 %copy-start = (f32[16,2048]{1,0:T(8,128)S(1)}, f32[16,2048]{1,0:T(8,128)}, u32[]{:S(2)}) copy-start(f32[16,2048]{1,0:T(8,128)} %latent_ref.1) | copy-start | bytes 393220

commit v4 on v2

--- a/solution.py
+++ b/solution.py
@@ -119,8 +119,8 @@
     latent_ref, te_ref, gain_ref, router_ref, up_hbm, down_hbm, routes_ref,
     out_ref,
     up_v, down_v, router_v, base, state, total,
-    take_first, take_second, spread, unpack, pack,
-    dsend, xbuf, ybuf, yrecv, zsend, rbuf,
+    take, spread, unpack, pack,
+    dsend, xbuf, wide, ybuf, yrecv, zsend, rbuf,
     w_sem, d_send, d_recv, n_send, n_recv, f_send, f_recv, y_send, y_recv, r_send, r_recv,
 ):
     nz, nc, layers, per_core, toks, width = sizes
@@ -170,14 +170,12 @@
         lane = lax.broadcasted_iota(jnp.int32, (rows, lanes), 1)
         return jnp.where(lane == target, 1.0, 0.0)
 
-    rows_in = srcs * PACK
-    per_block = srcs * CAP
-    i = lax.broadcasted_iota(jnp.int32, (rows_in, 1), 0)
-    unpack[...] = places(
-        rows_in, rows_in, (i % per_block) // CAP * PACK + i // per_block * CAP + i % CAP
-    ).astype(jnp.bfloat16)
+    per_half = half * CAP
     back = half * PACK
     i = lax.broadcasted_iota(jnp.int32, (back, 1), 0)
+    unpack[...] = places(
+        back, back, (i % per_half) // CAP * PACK + i // per_half * CAP + i % CAP
+    ).astype(jnp.bfloat16)
     pack[...] = places(
         back, back, (i % PACK) // CAP * (half * CAP) + i // PACK * CAP + i % CAP
     ).astype(jnp.bfloat16)
@@ -211,8 +209,8 @@
         block = lax.broadcasted_iota(jnp.int32, (BLOCKS * toks, 1), 0) // toks * CAP
         g0 = places(BLOCKS * toks, experts * PACK, jnp.concatenate([at_first] * BLOCKS, 0) + block)
         g1 = places(BLOCKS * toks, experts * PACK, jnp.concatenate([at_second] * BLOCKS, 0) + block)
-        take_first[p] = g0.astype(jnp.bfloat16)
-        take_second[p] = g1.astype(jnp.bfloat16)
+        take[p, :BLOCKS * toks] = g0.astype(jnp.bfloat16)
+        take[p, BLOCKS * toks:] = g1.astype(jnp.bfloat16)
         spread[p] = jnp.transpose(g0 + g1).astype(jnp.bfloat16)
         return carry
 
@@ -269,7 +267,7 @@
 
     def result_copy(j, h):
         return pltpu.make_async_remote_copy(
-            src_ref=ybuf.at[j, h, 1 - x],
+            src_ref=ybuf.at[j, h, 1],
             dst_ref=yrecv.at[j, h],
             send_sem=y_send.at[j, h],
             recv_sem=y_recv.at[j, h],
@@ -341,10 +339,24 @@
                     dispatch_copy(j, dz, dc, *came_from(dz, dc)).wait_recv()
                 forward_copy(j, dz, x).start()
 
+        def unpacked(j, place, side):
+            rows = jnp.dot(
+                unpack[...], xbuf[j, pl.ds(pl.multiple_of(side * back, back), back)],
+                preferred_element_type=jnp.float32,
+            ).astype(jnp.bfloat16)
+            for b in range(BLOCKS):
+                wide[j, place * per_half:(place + 1) * per_half, b * cols:(b + 1) * cols] = rows[
+                    b * per_half:(b + 1) * per_half
+                ]
+
         for j in range(per_core):
             for dz, dc in near:
                 if (dz, dc) != (0, 0):
                     dispatch_copy(j, dz, dc, *came_from(dz, dc)).wait_recv()
+            unpacked(j, 0, x)
+
+        for j in range(per_core):
+            for dz, dc in near:
                 near_copy(j, dz, dc, 1 - x, *came_from(dz, dc)).wait_recv()
             for dz in far:
                 forward_copy(j, dz, 1 - x).wait_recv()
@@ -354,14 +366,9 @@
                 for copy in weight_copies(layer, j):
                     copy.wait()
 
-            rows = jnp.dot(
-                unpack[...], xbuf[j], preferred_element_type=jnp.float32
-            ).astype(jnp.bfloat16)
-            wide = jnp.concatenate(
-                [rows[b * per_block:(b + 1) * per_block] for b in range(BLOCKS)], axis=1
-            )
+            unpacked(j, 1, 1 - x)
             acc = lax.dot_general(
-                wide, up_v[layer, j], (((1,), (1,)), ((), ())), preferred_element_type=jnp.float32
+                wide[j], up_v[layer, j], (((1,), (1,)), ((), ())), preferred_element_type=jnp.float32
             )
             hidden = jax.nn.gelu(acc, approximate=True).astype(jnp.bfloat16)
             for h in range(HALVES):
@@ -369,8 +376,8 @@
                     hidden, down_v[layer, j, :, h * part:(h + 1) * part],
                     preferred_element_type=jnp.float32,
                 ).astype(jnp.bfloat16)
-                ybuf[j, h, 0] = out[:per_block // 2]
-                ybuf[j, h, 1] = out[per_block // 2:]
+                ybuf[j, h, 0] = out[:per_half]
+                ybuf[j, h, 1] = out[per_half:]
                 result_copy(j, h).start()
 
         for j in range(per_core):
@@ -381,7 +388,7 @@
             for h in range(HALVES):
                 result_copy(j, h).wait_recv()
                 summed = (
-                    ybuf[j, h, x].astype(jnp.float32) + yrecv[j, h].astype(jnp.float32)
+                    ybuf[j, h, 0].astype(jnp.float32) + yrecv[j, h].astype(jnp.float32)
                 ).astype(jnp.bfloat16)
                 pieces += [summed[:, b * cols:(b + 1) * cols] for b in range(BLOCKS // HALVES)]
             tall = jnp.concatenate(pieces, axis=0)
@@ -406,8 +413,8 @@
             for dz, dc in others:
                 return_copy(j, dz, dc, *came_from(dz, dc)).wait_recv()
         returned = rbuf[...]
-        g0 = jnp.dot(take_first[p], returned, preferred_element_type=jnp.float32)
-        g1 = jnp.dot(take_second[p], returned, preferred_element_type=jnp.float32)
+        both = jnp.dot(take[p], returned, preferred_element_type=jnp.float32)
+        g0, g1 = both[:BLOCKS * toks], both[BLOCKS * toks:]
         for b in range(BLOCKS):
             r = slice(b * toks, (b + 1) * toks)
             w = slice(b * cols, (b + 1) * cols)
@@ -471,13 +478,13 @@
             pltpu.VMEM((toks, width), f32),
             pltpu.VMEM((toks, width), f32),
             pltpu.VMEM((toks, width), f32),
-            pltpu.VMEM((2 * layers, BLOCKS * toks, experts * PACK), bf16),
-            pltpu.VMEM((2 * layers, BLOCKS * toks, experts * PACK), bf16),
+            pltpu.VMEM((2 * layers, 2 * BLOCKS * toks, experts * PACK), bf16),
             pltpu.VMEM((2 * layers, experts * PACK, BLOCKS * toks), bf16),
-            pltpu.VMEM((srcs * PACK, srcs * PACK), bf16),
+            pltpu.VMEM((half * PACK, half * PACK), bf16),
             pltpu.VMEM((half * PACK, half * PACK), bf16),
             pltpu.VMEM((experts * PACK, cols), bf16),
             pltpu.VMEM((per_core, srcs * PACK, cols), bf16),
+            pltpu.VMEM((per_core, srcs * CAP, width), bf16),
             pltpu.VMEM((per_core, HALVES, 2, half * CAP, width // HALVES), bf16),
             pltpu.VMEM((per_core, HALVES, half * CAP, width // HALVES), bf16),
             pltpu.VMEM((per_core, half * PACK, cols), bf16),

time: 82.1 us -> 80.7 us (0.983)
  Pallas kernels: 79.6 us -> 78.3 us
    pallas_call x1, Pallas kernels: 79.6 us -> 78.3 us  [per_device(): pl.pallas_call(functools.partial(kernel, (nz, nc, layers, per_core, toks,...]
where the time goes in v4:
time: 80.7 us; the launch traced here: 80.5 us
  Pallas kernels  78.3 us (97%)
  other arithmetic  1.62 us (2%)
    pallas_call x1, Pallas kernels, per_device(): pl.pallas_call(functools.partial(kernel, (nz, nc, layers, per_core, toks,...  78.3 us
    mul x1, other arithmetic, per_device(): mean_velocity = 0.5 * total  1.62 us

profile of v4, /device:TPU:0, one launch (start us, length us, event | category | flops | bytes accessed | tf_op | source)
XLA Modules:
  0.0 80.5 jit_solution(6178951578569911975)
XLA Ops:
  0.6 0.0 copy-start
  0.6 78.3 %shard_map.86 = f32[16,2048]{1,0:T(8,128)} custom-call(f32[16,2048]{1,0:T(8,128)} %latent_ref.1, f32[1,2048]{1,0:T(1,128)} %bitcast.6, f32[2,2048]{1,0:T(2,128)} %gain_ref.1, f32[2,16,2048]{2,1,0:T(8,128)} %bitcast.5, bf16[2,4,704,2048]{3,2,1,0:T(8,128)(2,1)} %bitcast.4, bf16[2,4,704,2048]{3,2,1,0:T(8,128)(2,1)} %down_hbm.1, s32[2,2,2,16]{3,2,1,0:T(2,128)} %bitcast.7), custom_call_target="tpu_custom_call" | custom-call | flops 1476395008 | bytes 23068672 | tf_op jit(solution)/shard_map/pallas_call | solution.py:469
  78.9 0.0 copy-done
  78.9 1.6 %broadcast_multiply_fusion = (f32[16,2048]{1,0:T(8,128)}, f32[16,2048]{1,0:T(8,128)}) fusion(f32[16,2048]{1,0:T(8,128)} %shard_map.86, f32[16,2048]{1,0:T(8,128)S(1)} %copy-done), kind=kLoop, calls=%fused_computation.1 | loop fusion | flops 98304 | bytes 524288 | tf_op jit(solution)/shard_map/mul | solution.py:516
Async XLA Ops:
  0.6 78.3 %copy-start = (f32[16,2048]{1,0:T(8,128)S(1)}, f32[16,2048]{1,0:T(8,128)}, u32[]{:S(2)}) copy-start(f32[16,2048]{1,0:T(8,128)} %latent_ref.1) | copy-start | bytes 393220
